TPU v7x, 512 devices: a whole 4x8x8 slice. The times are simulated.
512 devices in a mesh: learn: 16 (over z, core), ep: 32 (over x, y).
Axes of the slice: x: 4, y: 8, z: 8, core: 2. Of those that a mesh axis runs over, the one named last changes fastest.
Arguments:
- master_weight: float32 [7168, 3, 32, 256], P(('learn', 'ep')), may hold values from -0.125 to 0.125
- gradient: bfloat16 [7168, 3, 32, 256], P(('learn', 'ep')), may hold values from -6 to 6
- first_moment: bfloat16 [7168, 3, 32, 256], P(('learn', 'ep')), may hold values from -1.5 to 1.5
- second_moment: bfloat16 [7168, 3, 32, 256], P(('learn', 'ep')), may hold values from 0.0099487305 to 0.29882812
- block_slot: int32 [32], replicated, may hold values from 0 to 31, each once
- queries: bfloat16 [2, 512, 32, 576], P(None, 'ep', 'learn'), may hold values from -512 to 512
- kv_cache: bfloat16 [512, 24, 576], P('ep'), may hold values from -512 to 512
- new_latent: bfloat16 [2, 512, 576], P(None, 'ep'), may hold values from -512 to 512
- lengths: int32 [512], P('ep'), may hold values from 1 to 24, 6144 in all
- uv_weight: bfloat16 [32, 512, 128], P('learn'), may hold values from -1 to 1
- out_weight: bfloat16 [32, 128, 7168], P('learn', None, 'ep'), may hold values from -0.09375 to 0.09375
- residual: bfloat16 [2, 512, 7168], P(None, ('learn', 'ep')), may hold values from -6 to 6
- norm_gain: float32 [7168], replicated, may hold values from 0.1 to 1.9
- expert_ids: int32 [2, 512, 8], P(None, ('learn', 'ep')), may hold values from 0 to 191, as said below
- route_weight: float32 [2, 512, 8], P(None, ('learn', 'ep')), may hold values from 0.05 to 1
Outputs:
- layer_out: bfloat16 [2, 512, 7168], P(None, ('learn', 'ep'))
Inputs may be any that keep to these rules, and one draw needn't show every extreme that they name: `block_slot`: each learner block is named once. `expert_ids`: each row names 8 different experts, two to four of them below 8.
All inputs are finite; a program needn't handle non-finite values. No bound on the sum of `lengths` on one device may be relied on, other than what follows from the above.
Results may differ from a plain program's by a relative error of at most 0.012.
Values may be sent and summed in bfloat16 or wider, within the bound.
A program may use at most 128 MiB of HBM per device.

v0:
```python
import jax
import jax.numpy as jnp
from jax import lax
from jax.sharding import PartitionSpec as P

BPE = 4
EXPERTS = 8
STEPS = 2


beta_one = 0.9
beta_two = 0.95
learn_rate = 0.01
adam_step = 50
adam_epsilon = 1e-08
norm_epsilon = 1e-06
route_scale = 2.827


def adam_update(master_weight, gradient, first_moment, second_moment):
    grad_value = gradient.astype(jnp.float32)
    first_new = beta_one * first_moment.astype(jnp.float32) + (1.0 - beta_one) * grad_value
    second_new = (
        beta_two * second_moment.astype(jnp.float32) + (1.0 - beta_two) * grad_value * grad_value
    )
    first_fix = 1.0 - beta_one**adam_step
    second_fix = 1.0 - beta_two**adam_step
    stride = first_new / first_fix / (jnp.sqrt(second_new / second_fix) + adam_epsilon)
    return (master_weight - learn_rate * stride).astype(jnp.bfloat16)


def invert_slot(block_slot):
    slot_count = block_slot.shape[0]
    order_ids = jnp.arange(slot_count)
    match_table = (block_slot[None, :] == order_ids[:, None]).astype(jnp.int32)
    return jnp.sum(match_table * order_ids[None, :], axis=1)


def attend_heads(query_rows, cache_rows, new_keys, lengths, uv_weight):
    key_rows = jnp.concatenate([cache_rows, new_keys], axis=1)
    key_count = key_rows.shape[1]
    latent_width = uv_weight.shape[1]
    score_scale = (uv_weight.shape[2] + key_rows.shape[2] - latent_width) ** (-0.5)
    position = jnp.arange(key_count)
    live_mask = (position[None, :] < lengths[:, None]) | (position[None, :] >= cache_rows.shape[1])
    scores = (
        jnp.einsum("rhk,rck->rhc", query_rows, key_rows, preferred_element_type=jnp.float32)
        * score_scale
    )
    scores = jnp.where(live_mask[:, None, :], scores, -1e30)
    row_max = jnp.max(scores, axis=2, keepdims=True)
    raised = jnp.exp(scores - row_max)
    soft_weight = (raised / jnp.sum(raised, axis=2, keepdims=True)).astype(jnp.bfloat16)
    latent = jnp.einsum(
        "rhc,rcl->rhl",
        soft_weight,
        key_rows[:, :, :latent_width],
        preferred_element_type=jnp.float32,
    ).astype(jnp.bfloat16)
    heads_out = jnp.einsum(
        "rhl,hlv->rhv", latent, uv_weight, preferred_element_type=jnp.float32
    ).astype(jnp.bfloat16)
    return heads_out.reshape(heads_out.shape[0], heads_out.shape[1] * heads_out.shape[2])


def scale_norm(hidden_state, norm_gain):
    spread_sq = jnp.mean(hidden_state * hidden_state, axis=-1, keepdims=True)
    return (hidden_state * lax.rsqrt(spread_sq + norm_epsilon) * norm_gain).astype(jnp.bfloat16)


def block_shares(expert_ids, route_weight):
    route_share = route_weight / jnp.sum(route_weight, axis=1, keepdims=True) * route_scale
    expert_index = jnp.arange(EXPERTS)
    hit_table = (expert_ids[:, :, None] == expert_index[None, None, :]).astype(jnp.float32)
    per_expert = jnp.sum(route_share[:, :, None] * hit_table, axis=1)
    return jnp.repeat(per_expert, BPE, axis=1)


def gate_terms(flat_rows, weights):
    width_in = weights.shape[0]
    pair_weights = weights[:, :2].reshape(width_in, 2 * weights.shape[2] * weights.shape[3])
    return jnp.dot(flat_rows, pair_weights, preferred_element_type=jnp.float32)


def activate(gate_up, weights):
    shaped = gate_up.reshape(gate_up.shape[0], 2, weights.shape[2], weights.shape[3])
    return (jax.nn.silu(shaped[:, 0]) * shaped[:, 1]).astype(jnp.bfloat16)


def down_project(activation, weights):
    produced = jnp.einsum(
        "rpb,dpb->rpd", activation, weights[:, 2], preferred_element_type=jnp.float32
    )
    return produced.astype(jnp.bfloat16)


def finish_block(gate_up, weights):
    return down_project(activate(gate_up, weights), weights)


def per_device(
    master_weight,
    gradient,
    first_moment,
    second_moment,
    block_slot,
    queries,
    kv_cache,
    new_latent,
    lengths,
    uv_weight,
    out_weight,
    residual,
    norm_gain,
    expert_ids,
    route_weight,
):
    owner_count = lax.axis_size("ep")
    updated = adam_update(master_weight, gradient, first_moment, second_moment)
    ordered = jnp.take(updated, invert_slot(block_slot), axis=2)
    owned = lax.all_to_all(ordered, "ep", split_axis=2, concat_axis=0, tiled=True)
    expert_weights = lax.all_gather(owned, "learn", axis=0, tiled=True)
    local_blocks = owned.shape[2]
    dim_model = norm_gain.shape[0]
    row_count = residual.shape[1]
    head_width = uv_weight.shape[0] * uv_weight.shape[2]
    col_count = out_weight.shape[2]
    out_flat = out_weight.reshape(head_width, col_count)
    results = []
    for decode_step in range(STEPS):
        new_keys = jnp.transpose(new_latent[: decode_step + 1], (1, 0, 2))
        heads_flat = attend_heads(queries[decode_step], kv_cache, new_keys, lengths, uv_weight)
        partial_value = jnp.dot(
            lax.all_gather(heads_flat, "ep", axis=0, tiled=True),
            out_flat,
            preferred_element_type=jnp.float32,
        )
        summed = lax.psum_scatter(partial_value, "learn", scatter_dimension=0, tiled=True).astype(
            jnp.bfloat16
        )
        spread = summed.reshape(owner_count, row_count, col_count)
        attended = lax.all_to_all(spread, "ep", split_axis=0, concat_axis=2, tiled=True).reshape(
            row_count, dim_model
        )
        hidden_state = residual[decode_step].astype(jnp.float32) + attended.astype(jnp.float32)
        normed = scale_norm(hidden_state, norm_gain)
        shares = block_shares(expert_ids[decode_step], route_weight[decode_step])
        shares_owner = shares.reshape(row_count, owner_count, local_blocks)
        used_owner = jnp.max(shares_owner, axis=2) > 0.0
        send_rows = jnp.where(
            jnp.transpose(used_owner)[:, :, None], normed[None, :, :], jnp.zeros((), jnp.bfloat16)
        )
        arrived = lax.all_to_all(send_rows, "ep", split_axis=0, concat_axis=0, tiled=True)
        item_count = arrived.shape[1]
        flat_rows = arrived.reshape(owner_count * item_count, dim_model)
        produced = finish_block(gate_terms(flat_rows, expert_weights), expert_weights)
        sent_back = produced.reshape(owner_count, item_count, local_blocks, dim_model)
        returned = lax.all_to_all(sent_back, "ep", split_axis=0, concat_axis=0, tiled=True)
        weighted = (
            returned.astype(jnp.float32) * jnp.transpose(shares_owner, (1, 0, 2))[:, :, :, None]
        )
        routed = jnp.sum(weighted, axis=(0, 2))
        results.append((hidden_state + routed).astype(jnp.bfloat16))
    return jnp.stack(results)


def solution(mesh):
    in_specs = (
        P(("learn", "ep"), None, None, None),
        P(("learn", "ep"), None, None, None),
        P(("learn", "ep"), None, None, None),
        P(("learn", "ep"), None, None, None),
        P(),
        P(None, "ep", "learn", None),
        P("ep", None, None),
        P(None, "ep", None),
        P("ep"),
        P("learn", None, None),
        P("learn", None, "ep"),
        P(None, ("learn", "ep"), None),
        P(),
        P(None, ("learn", "ep"), None),
        P(None, ("learn", "ep"), None),
    )
    out_specs = P(None, ("learn", "ep"), None)
    return jax.shard_map(
        per_device, mesh=mesh, in_specs=in_specs, out_specs=out_specs, check_vma=False
    )
```

profile of v0, /device:TPU:1, one launch (start us, length us, event | category | flops | bytes accessed | tf_op | source)
XLA Modules:
  0.0 360.9 jit_solution(7971605302789651071)
XLA Ops:
  7.4 3.1 fusion.17
  12.5 10.6 %all-to-all-start.1 = ((bf16[14,3,32,256]{3,0,1,2:T(8,128)(2,1)}), bf16[14,3,32,256]{3,0,1,2:T(8,128)(2,1)S(1)}, u32[]{:S(2)}, u32[]{:S(2)}) async-start(bf16[14,3,32,256]{3,0,1,2:T(8,128)(2,1)} %select_bitcast_fusion), calls=%async_computation.2 | async-start | bytes 1572864 | tf_op jit(solution)/shard_map/all_to_all | solution.py:121
  24.5 49.3 %all_gather.9 = bf16[512,256]{1,0:T(8,128)(2,1)S(1)} all-gather(bf16[16,256]{1,0:T(8,128)(2,1)S(1)} %bitcast.151), channel_id=1, replica_groups=mesh['learn'=16,'ep'=32] {'ep'}, dimensions={0}, use_global_device_ids=true | all-gather | bytes 270336 | tf_op jit(solution)/shard_map/all_gather | solution.py:134
  76.0 35.1 %all_gather.11 = bf16[512,256]{1,0:T(8,128)(2,1)S(1)} all-gather(bf16[16,256]{1,0:T(8,128)(2,1)S(1)} %bitcast.152), channel_id=1, replica_groups=mesh['learn'=16,'ep'=32] {'ep'}, dimensions={0}, use_global_device_ids=true | all-gather | bytes 270336 | tf_op jit(solution)/shard_map/all_gather | solution.py:134
  115.8 30.3 %reduce-scatter.3.cloned.1.call-done = f32[32,224]{1,0:T(8,128)} async-done(((f32[512,224]{1,0:T(8,128)}), f32[32,224]{1,0:T(8,128)}) %reduce-scatter.3.cloned.1.call-update) | async-done | bytes 28688 | tf_op jit(solution)/shard_map/reduce_scatter | solution.py:138
  147.6 9.1 %all-to-all-start = ((bf16[32,1,224]{2,1,0:T(2,128)(2,1)}), bf16[32,1,224]{2,1,0:T(2,128)(2,1)S(1)}, u32[]{:S(2)}, u32[]{:S(2)}) async-start(bf16[32,1,224]{2,1,0:T(2,128)(2,1)} %copy.107), calls=%async_computation.1 | async-start | bytes 65536 | tf_op jit(solution)/shard_map/all_to_all | solution.py:142
  156.7 50.3 %reduce-scatter.5.cloned.1.call-done = f32[32,224]{1,0:T(8,128)} async-done(((f32[512,224]{1,0:T(8,128)}), f32[32,224]{1,0:T(8,128)}) %reduce-scatter.5.cloned.1.call-update) | async-done | bytes 28688 | tf_op jit(solution)/shard_map/reduce_scatter | solution.py:138
  208.5 9.0 %all-to-all-start.4 = ((bf16[32,1,224]{2,1,0:T(2,128)(2,1)}), bf16[32,1,224]{2,1,0:T(2,128)(2,1)S(1)}, u32[]{:S(2)}, u32[]{:S(2)}) async-start(bf16[32,1,224]{2,1,0:T(2,128)(2,1)} %copy.116), calls=%async_computation.6 | async-start | bytes 65536 | tf_op jit(solution)/shard_map/all_to_all | solution.py:142
  217.8 8.5 %all-to-all-done.4 = bf16[32,1,224]{2,1,0:T(2,128)(2,1)S(1)} async-done(((bf16[32,1,224]{2,1,0:T(2,128)(2,1)}), bf16[32,1,224]{2,1,0:T(2,128)(2,1)S(1)}, u32[]{:S(2)}, u32[]{:S(2)}) %all-to-all-start.4) | async-done | bytes 14368 | tf_op jit(solution)/shard_map/all_to_all | solution.py:142
  229.8 3.5 reduce.18
  234.4 4.1 %all-to-all-start.2 = ((bf16[32,2,3584]{2,1,0:T(2,128)(2,1)}), bf16[32,2,3584]{2,1,0:T(2,128)(2,1)S(1)}, u32[]{:S(2)}, u32[]{:S(2)}) async-start(bf16[32,2,3584]{2,1,0:T(2,128)(2,1)} %reshape.688), calls=%async_computation.3 | async-start | bytes 917504 | tf_op jit(solution)/shard_map/all_to_all | solution.py:153
  239.1 3.5 reduce.20
  243.8 5.3 %all-to-all-done.2 = bf16[32,2,3584]{2,1,0:T(2,128)(2,1)S(1)} async-done(((bf16[32,2,3584]{2,1,0:T(2,128)(2,1)}), bf16[32,2,3584]{2,1,0:T(2,128)(2,1)S(1)}, u32[]{:S(2)}, u32[]{:S(2)}) %all-to-all-start.2) | async-done | bytes 458784 | tf_op jit(solution)/shard_map/all_to_all | solution.py:153
  249.1 5.6 %all-to-all-start.5 = ((bf16[32,2,3584]{2,1,0:T(2,128)(2,1)}), bf16[32,2,3584]{2,1,0:T(2,128)(2,1)S(1)}, u32[]{:S(2)}, u32[]{:S(2)}) async-start(bf16[32,2,3584]{2,1,0:T(2,128)(2,1)} %reshape.684), calls=%async_computation.7 | async-start | bytes 917504 | tf_op jit(solution)/shard_map/all_to_all | solution.py:153
  255.1 26.7 %all-gather.2.cloned.1.call-done = bf16[7168,3,1,256]{3,0,1,2:T(8,128)(2,1)} async-done(((bf16[448,3,1,256]{3,0,1,2:T(8,128)(2,1)}), bf16[7168,3,1,256]{3,0,1,2:T(8,128)(2,1)}) %all-gather.2.cloned.1.call-update) | async-done | bytes 11010064 | tf_op jit(solution)/shard_map/all_gather | solution.py:122
  281.8 6.5 %slice.74 = bf16[7168,2,1,256]{3,0,1,2:T(8,128)(2,1)} slice(bf16[7168,3,1,256]{3,0,1,2:T(8,128)(2,1)} %all-gather.2.cloned.1.call-done), slice={[0:7168], [0:2], [0:1], [0:256]} | slice | bytes 14680064 | tf_op jit(solution)/shard_map/slice | solution.py:81
  288.3 10.1 %copy.111 = bf16[7168,2,1,256]{0,3,1,2:T(8,128)(2,1)} copy(bf16[7168,2,1,256]{3,0,1,2:T(8,128)(2,1)} %slice.74) | data formatting | bytes 14680064 | tf_op jit(solution)/shard_map/slice | solution.py:81
  298.4 5.4 %fusion.18 = f32[32,2,1,256]{3,0,1,2:T(8,128)S(1)} fusion(bf16[7168,2,1,256]{0,3,1,2:T(8,128)(2,1)} %copy.111, bf16[32,1,7168]{2,1,0:T(2,128)(2,1)S(1)} %reshape.689), kind=kOutput, calls=%fused_computation.26 | convolution fusion | flops 234881024 | bytes 7864320 | tf_op jit(solution)/shard_map/dot_general | solution.py:82
  303.7 3.2 fusion.2
  309.0 9.3 %all-to-all-start.3 = ((bf16[32,2,3584]{2,1,0:T(2,128)(2,1)}), bf16[32,2,3584]{2,1,0:T(2,128)(2,1)S(1)}, u32[]{:S(2)}, u32[]{:S(2)}) async-start(bf16[32,2,3584]{2,1,0:T(2,128)(2,1)} %reshape.690), calls=%async_computation.4 | async-start | bytes 917504 | tf_op jit(solution)/shard_map/all_to_all | solution.py:158
  318.7 5.4 %fusion.21 = f32[32,2,1,256]{3,0,1,2:T(8,128)S(1)} fusion(bf16[7168,2,1,256]{0,3,1,2:T(8,128)(2,1)} %copy.111, bf16[32,1,7168]{2,1,0:T(2,128)(2,1)S(1)} %reshape.685), kind=kOutput, calls=%fused_computation.27 | convolution fusion | flops 234881024 | bytes 7864320 | tf_op jit(solution)/shard_map/dot_general | solution.py:82
  324.1 3.2 fusion.3
  331.4 8.0 %all-to-all-start.6 = ((bf16[32,2,3584]{2,1,0:T(2,128)(2,1)}), bf16[32,2,3584]{2,1,0:T(2,128)(2,1)S(1)}, u32[]{:S(2)}, u32[]{:S(2)}) async-start(bf16[32,2,3584]{2,1,0:T(2,128)(2,1)} %reshape.686), calls=%async_computation.8 | async-start | bytes 917504 | tf_op jit(solution)/shard_map/all_to_all | solution.py:158
  341.1 11.1 %all-to-all-done.6 = bf16[32,2,3584]{2,1,0:T(2,128)(2,1)S(1)} async-done(((bf16[32,2,3584]{2,1,0:T(2,128)(2,1)}), bf16[32,2,3584]{2,1,0:T(2,128)(2,1)S(1)}, u32[]{:S(2)}, u32[]{:S(2)}) %all-to-all-start.6) | async-done | bytes 458784 | tf_op jit(solution)/shard_map/all_to_all | solution.py:158
  (101 shorter events, 30.0 us)
Async XLA Ops:
  6.5 17.8 %copy-start = (bf16[2,512,128]{2,1,0:T(8,128)(2,1)S(1)}, bf16[2,512,128]{2,1,0:T(8,128)(2,1)}, u32[]{:S(2)}) copy-start(bf16[2,512,128]{2,1,0:T(8,128)(2,1)} %param.24) | copy-start | bytes 786436
  11.5 11.7 %copy-start.2 = (bf16[16,24,576]{2,1,0:T(8,128)(2,1)S(1)}, bf16[16,24,576]{2,1,0:T(8,128)(2,1)}, u32[]{:S(2)}) copy-start(bf16[16,24,576]{2,1,0:T(8,128)(2,1)} %param.21) | copy-start | bytes 1327108
  12.5 10.8 %copy-start.4 = (bf16[2,16,576]{2,1,0:T(8,128)(2,1)S(1)}, bf16[2,16,576]{2,1,0:T(8,128)(2,1)}, u32[]{:S(2)}) copy-start(bf16[2,16,576]{2,1,0:T(8,128)(2,1)} %param.22) | copy-start | bytes 110596
  12.5 10.9 %copy-start.7 = (s32[16]{0:T(128)S(1)}, s32[16]{0:T(128)}, u32[]{:S(2)}) copy-start(s32[16]{0:T(128)} %param.23) | copy-start | bytes 196
  12.5 11.0 %copy-start.9 = (bf16[2,16,2,576]{3,2,1,0:T(2,128)(2,1)S(1)}, bf16[2,16,2,576]{3,2,1,0:T(2,128)(2,1)}, u32[]{:S(2)}) copy-start(bf16[2,16,2,576]{3,2,1,0:T(2,128)(2,1)} %param.20) | copy-start | bytes 221188
  12.5 99.8 %all-to-all-start.1 = ((bf16[14,3,32,256]{3,0,1,2:T(8,128)(2,1)}), bf16[14,3,32,256]{3,0,1,2:T(8,128)(2,1)S(1)}, u32[]{:S(2)}, u32[]{:S(2)}) async-start(bf16[14,3,32,256]{3,0,1,2:T(8,128)(2,1)} %select_bitcast_fusion), calls=%async_computation.2 | async-start | bytes 1572864 | tf_op jit(solution)/shard_map/all_to_all | solution.py:121
  23.1 123.1 %reduce-scatter.3.cloned.1.call-start = ((), (), s32[]{:S(2)}) async-start(), calls=%async_computation.9 | async-start | bytes 557056 | tf_op jit(solution)/shard_map/reduce_scatter | solution.py:138
  23.3 50.5 %copy-start.3 = (bf16[2,128,224]{1,2,0:T(8,128)(2,1)S(1)}, bf16[2,128,224]{1,2,0:T(8,128)(2,1)}, u32[]{:S(2)}) copy-start(bf16[2,128,224]{1,2,0:T(8,128)(2,1)} %param.25) | copy-start | bytes 344068
  74.8 132.3 %reduce-scatter.5.cloned.1.call-start = ((), (), s32[]{:S(2)}) async-start(), calls=%async_computation.11 | async-start | bytes 557056 | tf_op jit(solution)/shard_map/reduce_scatter | solution.py:138
  112.2 169.6 %all-gather.2.cloned.1.call-start = ((), (), s32[]{:S(2)}) async-start(), calls=%async_computation.10 | async-start | bytes 11698176 | tf_op jit(solution)/shard_map/all_gather | solution.py:122
  112.3 1.1 copy-start.6
  112.3 1.7 copy-start.8
  112.4 3.4 copy-start.1
  112.4 116.2 %copy-start.5 = (f32[7168]{0:T(1024)S(1)}, f32[7168]{0:T(1024)}, u32[]{:S(2)}) copy-start(f32[7168]{0:T(1024)} %param.27) | copy-start | bytes 86020
  147.6 60.9 %all-to-all-start = ((bf16[32,1,224]{2,1,0:T(2,128)(2,1)}), bf16[32,1,224]{2,1,0:T(2,128)(2,1)S(1)}, u32[]{:S(2)}, u32[]{:S(2)}) async-start(bf16[32,1,224]{2,1,0:T(2,128)(2,1)} %copy.107), calls=%async_computation.1 | async-start | bytes 65536 | tf_op jit(solution)/shard_map/all_to_all | solution.py:142
  208.5 17.8 %all-to-all-start.4 = ((bf16[32,1,224]{2,1,0:T(2,128)(2,1)}), bf16[32,1,224]{2,1,0:T(2,128)(2,1)S(1)}, u32[]{:S(2)}, u32[]{:S(2)}) async-start(bf16[32,1,224]{2,1,0:T(2,128)(2,1)} %copy.116), calls=%async_computation.6 | async-start | bytes 65536 | tf_op jit(solution)/shard_map/all_to_all | solution.py:142
  234.4 14.7 %all-to-all-start.2 = ((bf16[32,2,3584]{2,1,0:T(2,128)(2,1)}), bf16[32,2,3584]{2,1,0:T(2,128)(2,1)S(1)}, u32[]{:S(2)}, u32[]{:S(2)}) async-start(bf16[32,2,3584]{2,1,0:T(2,128)(2,1)} %reshape.688), calls=%async_computation.3 | async-start | bytes 917504 | tf_op jit(solution)/shard_map/all_to_all | solution.py:153
  249.1 59.9 %all-to-all-start.5 = ((bf16[32,2,3584]{2,1,0:T(2,128)(2,1)}), bf16[32,2,3584]{2,1,0:T(2,128)(2,1)S(1)}, u32[]{:S(2)}, u32[]{:S(2)}) async-start(bf16[32,2,3584]{2,1,0:T(2,128)(2,1)} %reshape.684), calls=%async_computation.7 | async-start | bytes 917504 | tf_op jit(solution)/shard_map/all_to_all | solution.py:153
  309.0 22.4 %all-to-all-start.3 = ((bf16[32,2,3584]{2,1,0:T(2,128)(2,1)}), bf16[32,2,3584]{2,1,0:T(2,128)(2,1)S(1)}, u32[]{:S(2)}, u32[]{:S(2)}) async-start(bf16[32,2,3584]{2,1,0:T(2,128)(2,1)} %reshape.690), calls=%async_computation.4 | async-start | bytes 917504 | tf_op jit(solution)/shard_map/all_to_all | solution.py:158
  331.4 20.7 %all-to-all-start.6 = ((bf16[32,2,3584]{2,1,0:T(2,128)(2,1)}), bf16[32,2,3584]{2,1,0:T(2,128)(2,1)S(1)}, u32[]{:S(2)}, u32[]{:S(2)}) async-start(bf16[32,2,3584]{2,1,0:T(2,128)(2,1)} %reshape.686), calls=%async_computation.8 | async-start | bytes 917504 | tf_op jit(solution)/shard_map/all_to_all | solution.py:158
Sparse Core Ops, SparseCore 0:
  74.9 71.2 reduce-scatter.2
  149.2 57.8 reduce-scatter.4
  209.2 72.5 all-gather.1
where the time goes:
time: 365 us; the launch traced here: 361 us
  waiting for transfers between devices  134 us (37%)
  blocking collectives  84.4 us (23%)
  starting transfers between devices  55.8 us (15%)
  local copies, waits for them, and re-layouts  27.5 us (8%)
  other arithmetic  23 us (6%)
  matrix products  20.9 us (6%)
  between operations  14.8 us (4%)
    all_gather x2, blocking collectives, per_device(): lax.all_gather(heads_flat, 'ep', axis=0, tiled=True)  84.4 us
    reduce_scatter x2, waiting for transfers between devices, per_device(): lax.psum_scatter(partial_value, 'learn', scatter_dimension=0, tiled=True)  80.7 us
    all_gather x1, waiting for transfers between devices, per_device(): expert_weights = lax.all_gather(owned, 'learn', axis=0, tiled=True)  26.7 us
    all_to_all x2, starting transfers between devices, per_device(): lax.all_to_all(spread, 'ep', split_axis=0, concat_axis=2, tiled=True)  18.1 us
    all_to_all x2, starting transfers between devices, per_device(): lax.all_to_all(sent_back, 'ep', split_axis=0, concat_axis=0, tiled=True)  17.2 us
    slice x2, local copies, waits for them, and re-layouts, gate_terms(): weights[:, :2].reshape(width_in, 2 * weights.shape[2] * weights.shape[3])  16.6 us
    all_to_all x2, waiting for transfers between devices, per_device(): lax.all_to_all(sent_back, 'ep', split_axis=0, concat_axis=0, tiled=True)  13.2 us
    dot_general x2, matrix products, gate_terms(): return jnp.dot(flat_rows, pair_weights, preferred_element_type=jnp.float32)  10.7 us
  transfers between devices with their start and end apart: 10, of which 7 were waited for; matrix products, arithmetic and copies ran while one was open for 17% of the time, Pallas kernels for 0%

commit v1 on v0

v1 whole, which is shorter than its diff:
```python
import functools

import jax
import jax.numpy as jnp
from jax import lax
from jax.experimental import pallas as pl
from jax.experimental.pallas import tpu as pltpu
from jax.sharding import PartitionSpec as P

BF = jnp.bfloat16
F32 = jnp.float32
MESH = pl.DeviceIdType.MESH

beta_one = 0.9
beta_two = 0.95
learn_rate = 0.01
adam_step = 50
adam_epsilon = 1e-08
norm_epsilon = 1e-06
route_scale = 2.827

NX, NY, NZ, NL, NE = 4, 8, 8, 16, 32
WIDTH, SLICE, PART = 7168, 448, 224
LANES = 512
SS_LANE, SHARE_HI, SHARE_LO = 448, 456, 464
EXPERTS, STEPS, CACHE, LAT = 8, 2, 24, 512


def dot(a, b):
    return jnp.dot(a, b, preferred_element_type=F32)


def dot_t(a, b):
    return lax.dot_general(a, b, (((1,), (1,)), ((), ())), preferred_element_type=F32)


def iota(shape, dim):
    return lax.broadcasted_iota(jnp.int32, shape, dim)


def adam_kernel(slot_ref, mw_ref, gr_ref, fm_ref, sm_ref, out_ref, rows_ref):
    d = pl.program_id(0)

    @pl.when(d == 0)
    def _():
        rows_ref[...] = jnp.zeros_like(rows_ref)

    order = (slot_ref[...] == iota((NE, NE), 0)).astype(BF)
    first_fix = 1.0 - beta_one**adam_step
    second_fix = 1.0 - beta_two**adam_step
    for m in range(3):
        g = gr_ref[0, m].astype(F32)
        first_new = beta_one * fm_ref[0, m].astype(F32) + (1.0 - beta_one) * g
        second_new = beta_two * sm_ref[0, m].astype(F32) + (1.0 - beta_two) * g * g
        stride = first_new / first_fix / (jnp.sqrt(second_new / second_fix) + adam_epsilon)
        updated = (mw_ref[0, m] - learn_rate * stride).astype(BF)
        ordered = dot(order, updated)
        rows_ref[0, pl.ds(m * 16 + d, NE, stride=48), :] = ordered[:, :128]
        rows_ref[1, pl.ds(m * 16 + d, NE, stride=48), :] = ordered[:, 128:]

    @pl.when(d == pl.num_programs(0) - 1)
    def _():
        for half in range(2):
            out_ref[:, :, 128 * half : 128 * half + 128] = (
                rows_ref[half].reshape(NE, 48, 128).astype(BF)
            )


def adam_blocks(master_weight, gradient, first_moment, second_moment, block_slot):
    depth = master_weight.shape[0]
    spec = pl.BlockSpec((1, 3, NE, 256), lambda d: (d, 0, 0, 0))
    return pl.pallas_call(
        adam_kernel,
        grid=(depth,),
        out_shape=jax.ShapeDtypeStruct((NE, 48, 256), BF),
        in_specs=[pl.BlockSpec((1, NE), lambda d: (0, 0)), spec, spec, spec, spec],
        out_specs=pl.BlockSpec((NE, 48, 256), lambda d: (0, 0, 0)),
        scratch_shapes=[pltpu.VMEM((2, NE * 48, 128), F32)],
        compiler_params=pltpu.CompilerParams(vmem_limit_bytes=32 * 2**20),
        name="adam_blocks",
    )(block_slot.reshape(1, NE), master_weight, gradient, first_moment, second_moment)


def wait_bytes(ref, sem):
    pltpu.make_async_copy(ref, ref, sem).wait()


def remote(src, dst, ssem, rsem, device):
    return pltpu.make_async_remote_copy(
        src_ref=src, dst_ref=dst, send_sem=ssem, recv_sem=rsem, device_id=device, device_id_type=MESH
    )


def layer_kernel(
    q_ref, kk_ref, len_ref, uv_ref, ow_ref, res_ref, gain_ref, ws_ref, out_ref,
    heads, att_s, att_r, mov_s, mov_r, res_r, hid, rows, w_r, w_n,
    gate_s, gate_o, gate_r, sum_s, sum_r, sq_s, sq_r, sq_t, sq_z, acts, down_s, down_r,
    y_s, y_r, fin_s, fin_r, share,
    s_sem, r_sem, hy_sem, xy_sem,
):
    l = lax.axis_index("learn")
    e = lax.axis_index("ep")
    x, y = e // NY, lax.rem(e, NY)
    z, c = l // 2, lax.rem(l, 2)
    sib = {"learn": l + 1 - 2 * c}

    barrier = pltpu.get_barrier_semaphore()

    def greet_ep(k, carry):
        pl.semaphore_signal(barrier, inc=1, device_id={"ep": lax.rem(e + k, NE)}, device_id_type=MESH)
        return carry

    def greet_learn(k, carry):
        pl.semaphore_signal(barrier, inc=1, device_id={"learn": lax.rem(l + k, NL)}, device_id_type=MESH)
        return carry

    lax.fori_loop(1, NE, greet_ep, 0)
    lax.fori_loop(1, NL, greet_learn, 0)
    own_move = e // 2 == l
    for j in range(2):
        @pl.when(jnp.logical_not(jnp.logical_and(own_move, lax.rem(e, 2) == j)))
        def _():
            pl.semaphore_signal(
                barrier, inc=1, device_id={"learn": e // 2, "ep": 2 * l + j}, device_id_type=MESH
            )
    pl.semaphore_wait(barrier, NE - 1 + NL - 1 + 2 - own_move.astype(jnp.int32))

    res_r[l] = res_ref[l]

    def send_res(k, carry):
        t = lax.rem(l + k, NL)
        remote(res_ref.at[t], res_r.at[l], s_sem.at[0], r_sem.at[0], {"learn": t}).start()
        return carry

    lax.fori_loop(1, NL, send_res, 0)

    keys = kk_ref[...]
    scores = dot_t(q_ref[...], keys) * (192.0 ** (-0.5))
    shape = scores.shape
    row, col = iota(shape, 0), iota(shape, 1)
    row_i = lax.rem(row, 16)
    cached = 16 * CACHE
    first = row_i * CACHE
    live = jnp.logical_and(col >= first, col < first + len_ref[...])
    live = jnp.logical_or(live, col == cached + row_i)
    live = jnp.logical_or(live, jnp.logical_and(col == cached + 16 + row_i, row >= 32))
    scores = jnp.where(live, scores, -1e30)
    raised = jnp.exp(scores - jnp.max(scores, axis=1, keepdims=True))
    soft = (raised / jnp.sum(raised, axis=1, keepdims=True)).astype(BF)
    latent = dot(soft, keys[:, :LAT]).astype(BF)
    for s in range(STEPS):
        for h in range(2):
            start = s * 32 + h * 16
            heads[s, e, :, 128 * h : 128 * h + 128] = dot(
                latent[start : start + 16], uv_ref[h]
            ).astype(BF)

    def gather_start(buf, i, ysem, xsem):
        def send_y(k, carry):
            t = x * NY + lax.rem(y + k, NY)
            remote(buf.at[e], buf.at[e], s_sem.at[i], ysem.at[k], {"ep": t}).start()
            return carry

        def send_x(k, carry):
            t = lax.rem(x + k, NX) * NY + y
            remote(buf.at[e], buf.at[e], s_sem.at[i], xsem, {"ep": t}).start()
            return carry

        lax.fori_loop(1, NY, send_y, 0)
        lax.fori_loop(1, NX, send_x, 0)

    def gather_finish(buf, i, ysem, xsem):
        def relay(t, carry):
            half = t // 2
            k = jnp.where(lax.rem(t, 2) == 0, half + 1, NY - 1 - half)
            o = x * NY + lax.rem(y + NY - k, NY)
            wait_bytes(buf.at[o], ysem.at[k])

            def send_x(j, carry2):
                d = lax.rem(x + j, NX) * NY + y
                remote(buf.at[o], buf.at[o], s_sem.at[i], xsem, {"ep": d}).start()
                return carry2

            return lax.fori_loop(1, NX, send_x, carry)

        lax.fori_loop(0, NY - 1, relay, 0)
        wait_bytes(buf.at[pl.ds(0, NE - NY)], xsem)

    for s in range(STEPS):
        gather_start(heads.at[s], 1 + s, hy_sem.at[s], r_sem.at[1 + s])

    w_r[e] = ws_ref[e]

    def send_w(k, carry):
        t = lax.rem(e + k, NE)
        remote(ws_ref.at[t], w_r.at[e], s_sem.at[3], r_sem.at[3], {"ep": t}).start()
        return carry

    tokens = 512
    n, m = iota((tokens, tokens), 0), iota((tokens, tokens), 1)
    reorder = (m == 32 * lax.rem(n, 16) + n // 16).astype(BF)
    for s in range(STEPS):
        gather_finish(heads.at[s], 1 + s, hy_sem.at[s], r_sem.at[1 + s])
        ordered = dot(reorder, heads[s].reshape(tokens, 256)).astype(BF)
        att_s[s] = dot(ordered, ow_ref[...]).astype(BF).reshape(NL, 32, 256)
        att_r[s, l] = att_s[s, l]

        def send_att(k, carry):
            t = lax.rem(l + k, NL)
            remote(att_s.at[s, t], att_r.at[s, l], s_sem.at[4 + s], r_sem.at[4 + s], {"learn": t}).start()
            return carry

        lax.fori_loop(1, NL, send_att, 0)

    lax.fori_loop(1, NE, send_w, 0)

    for s in range(STEPS):
        wait_bytes(att_r.at[s, pl.ds(0, NL - 1)], r_sem.at[4 + s])
        total = att_r[s, 0].astype(F32)
        for k in range(1, NL):
            total = total + att_r[s, k].astype(F32)
        mov_s[s] = total.astype(BF).reshape(2, 16, 256)
        for j in range(2):
            here = jnp.logical_and(own_move, lax.rem(e, 2) == j)

            @pl.when(here)
            def _():
                mov_r[s, lax.rem(e, 2)] = mov_s[s, j]

            @pl.when(jnp.logical_not(here))
            def _():
                remote(
                    mov_s.at[s, j], mov_r.at[s, lax.rem(e, 2)], s_sem.at[6 + s], r_sem.at[6 + s],
                    {"learn": e // 2, "ep": 2 * l + j},
                ).start()

    def move_wait(s, sem):
        @pl.when(own_move)
        def _():
            wait_bytes(mov_r.at[s, 0], sem)

        @pl.when(jnp.logical_not(own_move))
        def _():
            wait_bytes(mov_r.at[s], sem)

    wait_bytes(res_r.at[pl.ds(0, NL - 1)], r_sem.at[0])
    lane = iota((16, LANES), 1)
    spread_row, spread_col = iota((256, LANES), 0), iota((256, LANES), 1)
    real = spread_row < PART
    place0 = jnp.logical_and(real, spread_col == spread_row).astype(BF)
    place1 = jnp.logical_and(real, spread_col == spread_row + PART).astype(BF)
    for s in range(STEPS):
        move_wait(s, r_sem.at[6 + s])
        attended = dot(mov_r[s, 0], place0) + dot(mov_r[s, 1], place1)
        value = res_r[:, s, :] + attended
        hid[s] = value
        squares = jnp.sum(jnp.where(lane < SLICE, value * value, 0.0), axis=1, keepdims=True)
        squares_hi = squares.astype(BF).astype(F32)
        value_hi = value.astype(BF).astype(F32)
        scaled = value * gain_ref[l]
        scaled = jnp.where(lane == SS_LANE, squares_hi, scaled)
        scaled = jnp.where(lane == SS_LANE + 1, squares - squares_hi, scaled)
        in_hi = jnp.logical_and(lane >= SHARE_HI, lane < SHARE_HI + EXPERTS)
        in_lo = jnp.logical_and(lane >= SHARE_LO, lane < SHARE_LO + EXPERTS)
        scaled = jnp.where(in_hi, value_hi, scaled)
        scaled = jnp.where(in_lo, value - value_hi, scaled)
        rows[s, e] = scaled.astype(BF)
        gather_start(rows.at[s], 8 + s, xy_sem.at[s], r_sem.at[8 + s])

    wait_bytes(w_r.at[pl.ds(0, NE - 1)], r_sem.at[3])
    pn, pm = iota((LANES, LANES), 0), iota((LANES, LANES), 1)
    pick = jnp.logical_and(pn < SLICE, pm == pn + 2 * (pn // 14)).astype(BF)
    for mat in range(3):
        natural = dot(pick, w_r[:, 16 * mat : 16 * mat + 16, :].reshape(LANES, 256)).astype(BF)
        if mat == 2:
            w_n[2] = natural
        else:
            for half in range(2):
                w_n[half, :, 128 * mat : 128 * mat + 128] = natural[:, 128 * half : 128 * half + 128]

    ones_at = iota((16, LANES), 1)
    stat_row = jnp.logical_or(ones_at == SS_LANE, ones_at == SS_LANE + 1).astype(BF)
    tail = iota((tokens, 128), 1) + 384
    mine = jnp.logical_or(tail == SHARE_HI + e // 4, tail == SHARE_LO + e // 4)
    for s in range(STEPS):
        gather_finish(rows.at[s], 8 + s, xy_sem.at[s], r_sem.at[8 + s])
        flat = rows[s].reshape(tokens, LANES)
        gate_s[s] = dot(flat, w_n[1 - c]).astype(BF)
        remote(gate_s.at[s], gate_r.at[s], s_sem.at[10 + s], r_sem.at[10 + s], sib).start()
        stat = dot_t(stat_row, flat)
        for t in range(4):
            sq_s[s, t] = stat[0:1, 128 * t : 128 * t + 128]
        remote(sq_s.at[s], sq_r.at[s], s_sem.at[12 + s], r_sem.at[12 + s], sib).start()
        gate_o[s] = dot(flat, w_n[c])
        share[s] = jnp.sum(jnp.where(mine, flat[:, 384:].astype(F32), 0.0), axis=1, keepdims=True)

    def z_peer(k):
        t = lax.rem(z + k, NZ)
        return t, {"learn": 2 * t + c}

    for s in range(STEPS):
        wait_bytes(gate_r.at[s], r_sem.at[10 + s])
        wait_bytes(sq_r.at[s], r_sem.at[12 + s])
        sum_s[s] = (gate_o[s] + gate_r[s].astype(F32)).astype(BF).reshape(NZ, 64, 256)
        sq_t[s] = sq_s[s] + sq_r[s]
        sum_r[s, z] = sum_s[s, z]
        sq_z[s, z] = sq_t[s, z // 2]

        def send_sum(k, carry):
            t, device = z_peer(k)
            remote(sq_t.at[s, t // 2], sq_z.at[s, z], s_sem.at[16 + s], r_sem.at[16 + s], device).start()
            remote(sum_s.at[s, t], sum_r.at[s, z], s_sem.at[14 + s], r_sem.at[14 + s], device).start()
            return carry

        lax.fori_loop(1, NZ, send_sum, 0)

    sq_row, sq_lane = iota((64, 128), 0), iota((64, 128), 1)
    own_lane = sq_lane == sq_row + 64 * lax.rem(z, 2)
    for s in range(STEPS):
        wait_bytes(sum_r.at[s, pl.ds(0, NZ - 1)], r_sem.at[14 + s])
        wait_bytes(sq_z.at[s, pl.ds(0, NZ - 1)], r_sem.at[16 + s])
        total = sum_r[s, 0].astype(F32)
        squares = sq_z[s, 0]
        for k in range(1, NZ):
            total = total + sum_r[s, k].astype(F32)
            squares = squares + sq_z[s, k]
        mean = jnp.sum(jnp.where(own_lane, squares, 0.0), axis=1, keepdims=True) / WIDTH
        total = total * lax.rsqrt(mean + norm_epsilon)
        gate, up = total[:, :128], total[:, 128:]
        acts[s, c, z] = (gate / (1.0 + jnp.exp(-gate)) * up).astype(BF)

        def send_act(k, carry):
            t, device = z_peer(k)
            remote(acts.at[s, c, z], acts.at[s, c, z], s_sem.at[18 + s], r_sem.at[18 + s], device).start()
            return carry

        lax.fori_loop(1, NZ, send_act, 0)

    for s in range(STEPS):
        wait_bytes(acts.at[s, c, pl.ds(0, NZ - 1)], r_sem.at[18 + s])
        remote(acts.at[s, c], acts.at[s, c], s_sem.at[20 + s], r_sem.at[20 + s], sib).start()

    for s in range(STEPS):
        wait_bytes(acts.at[s, 1 - c], r_sem.at[20 + s])
        act = jnp.concatenate(
            [acts[s, 0].reshape(tokens, 128), acts[s, 1].reshape(tokens, 128)], axis=1
        )
        down_s[s] = (dot_t(act, w_n[2]) * share[s]).astype(BF).reshape(NX, 128, LANES)
        down_r[s, x] = down_s[s, x]

        def send_down(k, carry):
            t = lax.rem(x + k, NX)
            remote(
                down_s.at[s, t], down_r.at[s, x], s_sem.at[22 + s], r_sem.at[22 + s], {"ep": t * NY + y}
            ).start()
            return carry

        lax.fori_loop(1, NX, send_down, 0)

    for s in range(STEPS):
        wait_bytes(down_r.at[s, pl.ds(0, NX - 1)], r_sem.at[22 + s])
        total = down_r[s, 0].astype(F32)
        for k in range(1, NX):
            total = total + down_r[s, k].astype(F32)
        y_s[s] = total.astype(BF).reshape(NY, 16, LANES)
        y_r[s, y] = y_s[s, y]

        def send_y(k, carry):
            t = lax.rem(y + k, NY)
            remote(
                y_s.at[s, t], y_r.at[s, y], s_sem.at[24 + s], r_sem.at[24 + s], {"ep": x * NY + t}
            ).start()
            return carry

        lax.fori_loop(1, NY, send_y, 0)

    for s in range(STEPS):
        wait_bytes(y_r.at[s, pl.ds(0, NY - 1)], r_sem.at[24 + s])
        total = hid[s]
        routed = y_r[s, 0].astype(F32)
        for k in range(1, NY):
            routed = routed + y_r[s, k].astype(F32)
        fin_s[:, s, :] = total + routed


    def send_fin(k, carry):
        t = lax.rem(l + k, NL)
        remote(fin_s.at[t], fin_r.at[l], s_sem.at[26], r_sem.at[26], {"learn": t}).start()
        return carry

    lax.fori_loop(1, NL, send_fin, 0)
    fin_r[l] = fin_s[l]
    wait_bytes(fin_r.at[pl.ds(0, NL - 1)], r_sem.at[26])
    out_ref[...] = fin_r[...]

    wait_bytes(res_r.at[pl.ds(0, NL - 1)], s_sem.at[0])
    wait_bytes(w_r.at[pl.ds(0, NE - 1)], s_sem.at[3])
    wait_bytes(fin_r.at[pl.ds(0, NL - 1)], s_sem.at[26])
    for s in range(STEPS):
        wait_bytes(heads.at[s, pl.ds(0, NE - 1)], s_sem.at[1 + s])
        wait_bytes(att_r.at[s, pl.ds(0, NL - 1)], s_sem.at[4 + s])
        move_wait(s, s_sem.at[6 + s])
        wait_bytes(rows.at[s, pl.ds(0, NE - 1)], s_sem.at[8 + s])
        wait_bytes(gate_s.at[s], s_sem.at[10 + s])
        wait_bytes(sq_s.at[s], s_sem.at[12 + s])
        wait_bytes(sum_s.at[s, pl.ds(0, NZ - 1)], s_sem.at[14 + s])
        wait_bytes(sq_z.at[s, pl.ds(0, NZ - 1)], s_sem.at[16 + s])
        wait_bytes(acts.at[s, 0, pl.ds(0, NZ - 1)], s_sem.at[18 + s])
        wait_bytes(acts.at[s, 0], s_sem.at[20 + s])
        wait_bytes(down_s.at[s, pl.ds(0, NX - 1)], s_sem.at[22 + s])
        wait_bytes(y_s.at[s, pl.ds(0, NY - 1)], s_sem.at[24 + s])


def layer(q, kk, lens, uv, ow, res, gain, ws):
    vmem = pl.BlockSpec(memory_space=pltpu.VMEM)
    scratch = [
        pltpu.VMEM((2, NE, 16, 256), BF),
        pltpu.VMEM((2, NL, 32, 256), BF),
        pltpu.VMEM((2, NL, 32, 256), BF),
        pltpu.VMEM((2, 2, 16, 256), BF),
        pltpu.VMEM((2, 2, 16, 256), BF),
        pltpu.VMEM((NL, 2, LANES), F32),
        pltpu.VMEM((2, 16, LANES), F32),
        pltpu.VMEM((2, NE, 16, LANES), BF),
        pltpu.VMEM((NE, 48, 256), BF),
        pltpu.VMEM((3, LANES, 256), BF),
        pltpu.VMEM((2, 512, 256), BF),
        pltpu.VMEM((2, 512, 256), F32),
        pltpu.VMEM((2, 512, 256), BF),
        pltpu.VMEM((2, NZ, 64, 256), BF),
        pltpu.VMEM((2, NZ, 64, 256), BF),
        pltpu.VMEM((2, 4, 1, 128), F32),
        pltpu.VMEM((2, 4, 1, 128), F32),
        pltpu.VMEM((2, 4, 1, 128), F32),
        pltpu.VMEM((2, NZ, 1, 128), F32),
        pltpu.VMEM((2, 2, NZ, 64, 128), BF),
        pltpu.VMEM((2, NX, 128, LANES), BF),
        pltpu.VMEM((2, NX, 128, LANES), BF),
        pltpu.VMEM((2, NY, 16, LANES), BF),
        pltpu.VMEM((2, NY, 16, LANES), BF),
        pltpu.VMEM((NL, 2, LANES), F32),
        pltpu.VMEM((NL, 2, LANES), F32),
        pltpu.VMEM((2, 512, 1), F32),
        pltpu.SemaphoreType.DMA((27,)),
        pltpu.SemaphoreType.DMA((27,)),
        pltpu.SemaphoreType.DMA((2, NY)),
        pltpu.SemaphoreType.DMA((2, NY)),
    ]
    return pl.pallas_call(
        layer_kernel,
        out_shape=jax.ShapeDtypeStruct((NL, 2, LANES), F32),
        in_specs=[vmem] * 8,
        out_specs=vmem,
        scratch_shapes=scratch,
        compiler_params=pltpu.CompilerParams(
            collective_id=0, has_side_effects=True, vmem_limit_bytes=48 * 2**20
        ),
        name="decode_layer",
    )(q, kk, lens, uv, ow, res, gain, ws)


def expert_shares(expert_ids, route_weight):
    route_share = route_weight / jnp.sum(route_weight, axis=-1, keepdims=True) * route_scale
    hit = (expert_ids[..., None] == jnp.arange(EXPERTS)).astype(F32)
    return jnp.sum(route_share[..., None] * hit, axis=-2)


def per_device(
    master_weight, gradient, first_moment, second_moment, block_slot, queries, kv_cache, new_latent,
    lengths, uv_weight, out_weight, residual, norm_gain, expert_ids, route_weight,
):
    ws = adam_blocks(master_weight, gradient, first_moment, second_moment, block_slot)
    q = jnp.transpose(queries, (0, 2, 1, 3)).reshape(64, 576)
    kk = jnp.concatenate([kv_cache.reshape(16 * CACHE, 576), new_latent.reshape(32, 576)], axis=0)
    lens = jnp.tile(lengths, 4).reshape(64, 1)
    ow = jnp.pad(out_weight.reshape(256, PART), ((0, 0), (0, 256 - PART)))
    shares = expert_shares(expert_ids[:, 0], route_weight[:, 0])
    gap = jnp.zeros((2, 8), F32)
    tail = jnp.concatenate([gap, shares, shares, gap, gap, gap, gap, gap], axis=1)
    res = jnp.concatenate(
        [
            jnp.transpose(residual.astype(F32).reshape(2, NL, SLICE), (1, 0, 2)),
            jnp.broadcast_to(tail[None], (NL, 2, LANES - SLICE)),
        ],
        axis=2,
    )
    gain = jnp.pad(norm_gain.reshape(NL, 1, SLICE), ((0, 0), (0, 0), (0, LANES - SLICE)))
    out = layer(q, kk, lens, uv_weight, ow, res, gain, ws)
    return jnp.transpose(out[:, :, :SLICE], (1, 0, 2)).reshape(2, 1, WIDTH).astype(BF)


def solution(mesh):
    in_specs = (
        P(("learn", "ep"), None, None, None),
        P(("learn", "ep"), None, None, None),
        P(("learn", "ep"), None, None, None),
        P(("learn", "ep"), None, None, None),
        P(),
        P(None, "ep", "learn", None),
        P("ep", None, None),
        P(None, "ep", None),
        P("ep"),
        P("learn", None, None),
        P("learn", None, "ep"),
        P(None, ("learn", "ep"), None),
        P(),
        P(None, ("learn", "ep"), None),
        P(None, ("learn", "ep"), None),
    )
    out_specs = P(None, ("learn", "ep"), None)
    return jax.shard_map(
        per_device, mesh=mesh, in_specs=in_specs, out_specs=out_specs, check_vma=False
    )
```

time: 365 us -> 135 us (0.37)
  waiting for transfers between devices: 134 us -> 0 us
  Pallas kernels: 0 us -> 123 us
  blocking collectives: 84.4 us -> 0 us
  starting transfers between devices: 55.8 us -> 0 us
  matrix products: 20.9 us -> 0 us
  local copies, waits for them, and re-layouts: 27.5 us -> 7.62 us
  other arithmetic: 23 us -> 3.56 us
  between operations: 14.8 us -> 0.16 us
    pallas_call x0 -> x2, Pallas kernels: none -> 123 us  [the longest x1 120 us: layer(): pl.pallas_call(layer_kernel, out_shape=jax.ShapeDtypeStruct((NL, 2, LANES...]
    all_gather x2 -> x0, blocking collectives: 84.4 us -> none  [per_device(): lax.all_gather(heads_flat, 'ep', axis=0, tiled=True)]
    reduce_scatter x2 -> x0, waiting for transfers between devices: 80.7 us -> none  [per_device(): lax.psum_scatter(partial_value, 'learn', scatter_dimension=0, tiled=True)]
    all_to_all x7 -> x0, starting transfers between devices: 55.7 us -> none  [the longest x2 18.1 us: per_device(): lax.all_to_all(spread, 'ep', split_axis=0, concat_axis=2, tiled=True)]
    all_to_all x7 -> x0, waiting for transfers between devices: 27 us -> none  [the longest x2 13.2 us: per_device(): lax.all_to_all(sent_back, 'ep', split_axis=0, concat_axis=0, tiled=True)]
    all_gather x1 -> x0, waiting for transfers between devices: 26.7 us -> none  [per_device(): expert_weights = lax.all_gather(owned, 'learn', axis=0, tiled=True)]
    dot_general x12 -> x0, matrix products: 20.9 us -> none  [the longest x2 10.7 us: gate_terms(): return jnp.dot(flat_rows, pair_weights, preferred_element_type=jnp.float32)]
    slice x2 -> x0, local copies, waits for them, and re-layouts: 16.6 us -> none  [gate_terms(): weights[:, :2].reshape(width_in, 2 * weights.shape[2] * weights.shape[3])]
  transfers between devices with their start and end apart: 10 -> 0, of which waited for: 7 -> 0; matrix products, arithmetic and copies ran while one was open for 17% -> 0% of each run, Pallas kernels for 0% -> 0%
where the time goes in v1:
time: 135 us; the launch traced here: 134 us
  Pallas kernels  123 us (91%)
  local copies, waits for them, and re-layouts  7.62 us (6%)
  other arithmetic  3.56 us (3%)
    pallas_call x1, Pallas kernels, layer(): pl.pallas_call(layer_kernel, out_shape=jax.ShapeDtypeStruct((NL, 2, LANES...  120 us
    pallas_call x1, Pallas kernels, adam_blocks(): pl.pallas_call(adam_kernel, grid=(depth,), out_shape=jax.ShapeDtypeStruct...  3.54 us
    unnamed x15, local copies, waits for them, and re-layouts  3.22 us

profile of v1, /device:TPU:1, one launch (start us, length us, event | category | flops | bytes accessed | tf_op | source)
XLA Modules:
  0.0 134.5 jit_solution(9899338070500459375)
XLA Ops:
  0.0 0.8 reduce_sum.18
  0.8 0.8 divide_multiply_fusion
  1.5 0.8 select_reduce_fusion
  2.3 0.1 pad.15.clone
  2.4 0.1 maximum_maximum_fusion
  2.5 0.7 tile.2
  3.1 0.1 reshape_tile.4.len_ref
  3.2 0.8 reshape.65
  4.1 0.0 copy-start
  4.1 0.0 copy-start.1
  4.1 0.0 copy-start.5
  4.1 1.0 reshape.67
  5.1 0.1 copy.30
  5.2 0.1 pad_maximum_fusion.1.res_ref
  5.3 0.9 copy.24
  6.2 1.0 copy.25
  7.2 0.0 copy-done.6
  7.2 1.1 pad_maximum_fusion.kk_ref
  8.3 0.0 copy-start.2
  8.4 1.1 copy-done.2
  9.4 1.1 copy-done.3
  10.5 3.5 %adam_blocks.1.ws_ref = bf16[32,48,256]{2,1,0:T(8,128)(2,1)S(1)} custom-call(s32[1,32]{1,0:T(1,128)S(1)} %bitcast.16, f32[14,3,32,256]{3,2,1,0:T(8,128)S(1)} %copy-done, bf16[14,3,32,256]{3,2,1,0:T(8,128)(2,1)S(1)} %copy-done.1, bf16[14,3,32,256]{3,2,1,0:T(8,128)(2,1)S(1)} %copy-done.2, bf16[14,3,32,256]{3,2,1,0:T(8,128)(2,1)S(1)} %copy-done.3), custom_call_target="tpu_custom_call" | custom-call | tf_op jit(solution)/shard_map/adam_blocks/pallas_call | solution.py:72
  14.1 119.6 %decode_layer.1 = f32[16,2,512]{2,1,0:T(2,128)S(1)} custom-call(bf16[64,576]{1,0:T(8,128)(2,1)S(1)} %bitcast.15, bf16[416,576]{1,0:T(8,128)(2,1)S(1)} %pad_maximum_fusion.kk_ref, s32[64,1]{1,0:T(8,128)S(1)} %reshape_tile.4.len_ref, bf16[2,512,128]{2,1,0:T(8,128)(2,1)S(1)} %copy-done.4, bf16[256,256]{1,0:T(8,128)(2,1)S(1)} %pad.8.ow_ref, ...), custom_call_target="tpu_custom_call" | custom-call | tf_op jit(solution)/shard_map/decode_layer/pallas_call | solution.py:449
  133.7 0.7 convert_element_type.22
  (15 shorter events, 0.1 us)
Async XLA Ops:
  0.0 7.2 %copy-start.6 = (bf16[2,16,576]{2,1,0:T(8,128)(2,1)S(1)}, bf16[2,16,576]{2,1,0:T(8,128)(2,1)}, u32[]{:S(2)}) copy-start(bf16[2,16,576]{2,1,0:T(8,128)(2,1)} %param.22) | copy-start | bytes 110596
  4.1 4.2 %copy-start = (f32[14,3,32,256]{3,2,1,0:T(8,128)S(1)}, f32[14,3,32,256]{3,2,1,0:T(8,128)}, u32[]{:S(2)}) copy-start(f32[14,3,32,256]{3,2,1,0:T(8,128)} %mw_ref.1) | copy-start | bytes 4128772
  4.1 4.2 %copy-start.1 = (bf16[14,3,32,256]{3,2,1,0:T(8,128)(2,1)S(1)}, bf16[14,3,32,256]{3,2,1,0:T(8,128)(2,1)}, u32[]{:S(2)}) copy-start(bf16[14,3,32,256]{3,2,1,0:T(8,128)(2,1)} %gr_ref.1) | copy-start | bytes 2064388
  4.1 4.2 %copy-start.5 = (s32[32]{0:T(128)S(1)}, s32[32]{0:T(128)}, u32[]{:S(2)}) copy-start(s32[32]{0:T(128)} %param.19) | copy-start | bytes 388
  8.3 1.1 copy-start.2
  9.4 1.1 copy-start.3
  10.5 3.6 %copy-start.4 = (bf16[2,512,128]{2,1,0:T(8,128)(2,1)S(1)}, bf16[2,512,128]{2,1,0:T(8,128)(2,1)}, u32[]{:S(2)}) copy-start(bf16[2,512,128]{2,1,0:T(8,128)(2,1)} %uv_ref.1) | copy-start | bytes 786436

commit v2 on v1

v2 whole, which is shorter than its diff:
```python
import functools

import jax
import jax.numpy as jnp
from jax import lax
from jax.experimental import pallas as pl
from jax.experimental.pallas import tpu as pltpu
from jax.sharding import PartitionSpec as P

BF = jnp.bfloat16
F32 = jnp.float32
MESH = pl.DeviceIdType.MESH

beta_one = 0.9
beta_two = 0.95
learn_rate = 0.01
adam_step = 50
adam_epsilon = 1e-08
norm_epsilon = 1e-06
route_scale = 2.827

NX, NY, NZ, NL, NE = 4, 8, 8, 16, 32
WIDTH, SLICE, PART = 7168, 448, 224
LANES = 512
SS_LANE, SHARE_HI, SHARE_LO = 448, 456, 464
EXPERTS, STEPS, CACHE, LAT = 8, 2, 24, 512


def dot(a, b):
    return jnp.dot(a, b, preferred_element_type=F32)


def dot_t(a, b):
    return lax.dot_general(a, b, (((1,), (1,)), ((), ())), preferred_element_type=F32)


def iota(shape, dim):
    return lax.broadcasted_iota(jnp.int32, shape, dim)


def wait_bytes(ref, sem):
    pltpu.make_async_copy(ref, ref, sem).wait()


def remote(src, dst, ssem, rsem, device):
    return pltpu.make_async_remote_copy(
        src_ref=src, dst_ref=dst, send_sem=ssem, recv_sem=rsem, device_id=device, device_id_type=MESH
    )


def column(row, size):
    count = row.shape[1]
    hit = lax.rem(iota((size, count), 0), count) == iota((size, count), 1)
    return jnp.sum(jnp.where(hit, row, jnp.zeros_like(row)), axis=1, keepdims=True)


def layer_kernel(
    mw_in, gr_in, fm_in, sm_in, slot_in, q_in, kv_in, new_in, len_in, uv_in, ow_in,
    residual_in, gain_in, ids_in, route_in, out_ref,
    mw, gr, fm, sm, slot_ref, q_ref, kv_ref, new_ref, len_ref, uv_ref, ow_ref,
    residual_ref, gain_ref, ids_ref, route_ref,
    w_s, heads, att_s, att_r, mov_s, mov_r, res_s, res_r, hid, rows, w_r, w_n,
    gate_s, gate_o, gate_r, sum_s, sum_r, sq_s, sq_r, sq_t, sq_z, acts, down_s, down_r,
    y_s, y_r, fin_s, fin_r, share,
    s_sem, r_sem, hy_sem, xy_sem, down_sem, l_sem,
):
    l = lax.axis_index("learn")
    e = lax.axis_index("ep")
    x, y = e // NY, lax.rem(e, NY)
    z, c = l // 2, lax.rem(l, 2)
    sib = {"learn": l + 1 - 2 * c}

    pairs = (
        (q_in, q_ref), (kv_in, kv_ref), (new_in, new_ref), (len_in, len_ref), (uv_in, uv_ref),
        (residual_in, residual_ref), (ids_in, ids_ref), (route_in, route_ref), (ow_in, ow_ref),
        (slot_in, slot_ref), (gain_in, gain_ref), (mw_in, mw), (gr_in, gr), (fm_in, fm), (sm_in, sm),
    )
    loads = [pltpu.make_async_copy(src, dst, l_sem.at[i]) for i, (src, dst) in enumerate(pairs)]
    for load in loads[:11]:
        load.start()

    barrier = pltpu.get_barrier_semaphore()

    def greet_ep(k, carry):
        pl.semaphore_signal(barrier, inc=1, device_id={"ep": lax.rem(e + k, NE)}, device_id_type=MESH)
        return carry

    def greet_learn(k, carry):
        pl.semaphore_signal(barrier, inc=1, device_id={"learn": lax.rem(l + k, NL)}, device_id_type=MESH)
        return carry

    lax.fori_loop(1, NE, greet_ep, 0)
    lax.fori_loop(1, NL, greet_learn, 0)
    own_move = e // 2 == l
    for j in range(2):
        @pl.when(jnp.logical_not(jnp.logical_and(own_move, lax.rem(e, 2) == j)))
        def _():
            pl.semaphore_signal(
                barrier, inc=1, device_id={"learn": e // 2, "ep": 2 * l + j}, device_id_type=MESH
            )

    for load in loads[:5]:
        load.wait()
    for load in loads[11:]:
        load.start()

    cached = 16 * CACHE
    scale = 192.0 ** (-0.5)
    parts = []
    for s in range(STEPS):
        wide = q_ref[s].astype(F32)
        for h in range(2):
            parts.append(wide[:, h, :].astype(BF))
    q = jnp.concatenate(parts, axis=0)
    old, new = kv_ref[...], new_ref[...]
    old_score, new_score = dot_t(q, old) * scale, dot_t(q, new) * scale
    row, col = iota((64, cached), 0), iota((64, cached), 1)
    first = lax.rem(row, 16) * CACHE
    live = jnp.logical_and(col >= first, col < first + column(len_ref[...], 64))
    old_score = jnp.where(live, old_score, -1e30)
    row, col = iota((64, 32), 0), iota((64, 32), 1)
    live = jnp.logical_and(lax.rem(row, 16) == lax.rem(col, 16), jnp.logical_or(col < 16, row >= 32))
    new_score = jnp.where(live, new_score, -1e30)
    top = jnp.maximum(
        jnp.max(old_score, axis=1, keepdims=True), jnp.max(new_score, axis=1, keepdims=True)
    )
    old_score, new_score = jnp.exp(old_score - top), jnp.exp(new_score - top)
    norm = jnp.sum(old_score, axis=1, keepdims=True) + jnp.sum(new_score, axis=1, keepdims=True)
    latent = dot((old_score / norm).astype(BF), old[:, :LAT])
    latent = (latent + dot((new_score / norm).astype(BF), new[:, :LAT])).astype(BF)
    for s in range(STEPS):
        for h in range(2):
            start = s * 32 + h * 16
            heads[s, e, :, 128 * h : 128 * h + 128] = dot(
                latent[start : start + 16], uv_ref[h]
            ).astype(BF)

    def gather_start(buf, i, ysem, xsem):
        def send_y(k, carry):
            t = x * NY + lax.rem(y + k, NY)
            remote(buf.at[e], buf.at[e], s_sem.at[i], ysem.at[k], {"ep": t}).start()
            return carry

        def send_x(k, carry):
            t = lax.rem(x + k, NX) * NY + y
            remote(buf.at[e], buf.at[e], s_sem.at[i], xsem, {"ep": t}).start()
            return carry

        lax.fori_loop(1, NY, send_y, 0)
        lax.fori_loop(1, NX, send_x, 0)

    def gather_relay(buf, i, ysem, xsem):
        def relay(t, carry):
            half = t // 2
            k = jnp.where(lax.rem(t, 2) == 0, half + 1, NY - 1 - half)
            o = x * NY + lax.rem(y + NY - k, NY)
            wait_bytes(buf.at[o], ysem.at[k])

            def send_x(j, carry2):
                d = lax.rem(x + j, NX) * NY + y
                remote(buf.at[o], buf.at[o], s_sem.at[i], xsem, {"ep": d}).start()
                return carry2

            return lax.fori_loop(1, NX, send_x, carry)

        lax.fori_loop(0, NY - 1, relay, 0)

    def heads_start(s):
        gather_start(heads.at[s], 1 + s, hy_sem.at[s], r_sem.at[1 + s])

    pl.semaphore_wait(barrier, NE - 1 + NL - 1 + 2 - own_move.astype(jnp.int32))
    for s in range(STEPS):
        heads_start(s)

    for load in loads[5:]:
        load.wait()
    lane8 = iota((8, LANES - SLICE), 1)
    hi_expert, lo_expert = lane8 - (SHARE_HI - SLICE), lane8 - (SHARE_LO - SLICE)
    tails = []
    for s in range(STEPS):
        ids = column(ids_ref[s], 8)
        weight = route_ref[s]
        route = column(weight / jnp.sum(weight, axis=1, keepdims=True) * route_scale, 8)
        hit = jnp.logical_or(
            jnp.logical_and(ids == hi_expert, hi_expert < EXPERTS),
            jnp.logical_and(ids == lo_expert, lo_expert < EXPERTS),
        )
        tails.append(jnp.sum(jnp.where(hit, route, 0.0), axis=0, keepdims=True))
    tail = jnp.concatenate(tails, axis=0)
    lines = residual_ref[...].astype(F32)
    for k in range(NL):
        res_s[k] = jnp.concatenate([lines[:, SLICE * k : SLICE * k + SLICE], tail], axis=1)
    res_r[l] = res_s[l]

    def send_res(k, carry):
        t = lax.rem(l + k, NL)
        remote(res_s.at[t], res_r.at[l], s_sem.at[0], r_sem.at[0], {"learn": t}).start()
        return carry

    lax.fori_loop(1, NL, send_res, 0)

    depth = mw.shape[0]
    count = depth * NE
    slots = column(slot_ref[...], NE).astype(F32)
    fits = lax.rem(iota((NE, count), 1), NE) == iota((NE, count), 0)
    slot_row = jnp.sum(jnp.where(fits, slots, 0.0), axis=0, keepdims=True).astype(jnp.int32)
    out_row, in_row = iota((NE * 16, count), 0), iota((NE * 16, count), 1)
    order = jnp.logical_and(out_row // 16 == slot_row, lax.rem(out_row, 16) == in_row // NE).astype(BF)
    first_scale = learn_rate / (1.0 - beta_one**adam_step)
    second_scale = 1.0 / (1.0 - beta_two**adam_step)
    for mat in range(3):
        g = gr[:, mat].astype(F32)
        first_new = beta_one * fm[:, mat].astype(F32) + (1.0 - beta_one) * g
        second_new = beta_two * sm[:, mat].astype(F32) + (1.0 - beta_two) * g * g
        stride = first_new * first_scale / (jnp.sqrt(second_new * second_scale) + adam_epsilon)
        updated = (mw[:, mat] - stride).astype(BF).reshape(count, 256)
        w_s[:, 16 * mat : 16 * mat + 16, :] = dot(order, updated).reshape(NE, 16, 256).astype(BF)

    w_r[e] = w_s[e]

    def send_w(k, carry):
        t = lax.rem(e + k, NE)
        remote(w_s.at[t], w_r.at[e], s_sem.at[3], r_sem.at[3], {"ep": t}).start()
        return carry

    tokens = 512
    n, m = iota((tokens, tokens), 0), iota((tokens, tokens), 1)
    reorder = (m == 32 * lax.rem(n, 16) + n // 16).astype(BF)

    def heads_relay(s):
        gather_relay(heads.at[s], 1 + s, hy_sem.at[s], r_sem.at[1 + s])

    def project(s):
        wait_bytes(heads.at[s, pl.ds(0, NE - NY)], r_sem.at[1 + s])
        ordered = dot(reorder, heads[s].reshape(tokens, 256)).astype(BF)
        projected = dot_t(ordered[:, :128], ow_ref[0]) + dot_t(ordered[:, 128:], ow_ref[1])
        att_s[s] = projected.astype(BF).reshape(NL, 32, PART)
        att_r[s, l] = att_s[s, l]

        def send_att(k, carry):
            t = lax.rem(l + k, NL)
            remote(att_s.at[s, t], att_r.at[s, l], s_sem.at[4 + s], r_sem.at[4 + s], {"learn": t}).start()
            return carry

        lax.fori_loop(1, NL, send_att, 0)

    def move(s):
        wait_bytes(att_r.at[s, pl.ds(0, NL - 1)], r_sem.at[4 + s])
        total = att_r[s, 0].astype(F32)
        for k in range(1, NL):
            total = total + att_r[s, k].astype(F32)
        mov_s[s] = total.astype(BF).reshape(2, 16, PART)
        for j in range(2):
            here = jnp.logical_and(own_move, lax.rem(e, 2) == j)

            @pl.when(here)
            def _():
                mov_r[s, lax.rem(e, 2)] = mov_s[s, j]

            @pl.when(jnp.logical_not(here))
            def _():
                remote(
                    mov_s.at[s, j], mov_r.at[s, lax.rem(e, 2)], s_sem.at[6 + s], r_sem.at[6 + s],
                    {"learn": e // 2, "ep": 2 * l + j},
                ).start()

    def move_wait(s, sem):
        @pl.when(own_move)
        def _():
            wait_bytes(mov_r.at[s, 0], sem)

        @pl.when(jnp.logical_not(own_move))
        def _():
            wait_bytes(mov_r.at[s], sem)

    gains = gain_ref[pl.ds(7 * z, 7), :]
    even = jnp.concatenate([gains[k : k + 1] for k in range(4)], axis=1)
    odd = jnp.concatenate([gains[k : k + 1] for k in range(3, 7)], axis=1)
    odd = jnp.concatenate([odd[:, 64:], odd[:, :64]], axis=1)
    gain = jnp.where(c == 0, even, odd)
    lane = iota((16, LANES), 1)
    spread_row, spread_col = iota((PART, LANES), 0), iota((PART, LANES), 1)
    place0 = (spread_col == spread_row).astype(BF)
    place1 = (spread_col == spread_row + PART).astype(BF)

    def rows_start(s):
        move_wait(s, r_sem.at[6 + s])
        attended = dot(mov_r[s, 0], place0) + dot(mov_r[s, 1], place1)
        value = res_r[:, s, :] + attended
        hid[s] = value
        squares = jnp.sum(jnp.where(lane < SLICE, value * value, 0.0), axis=1, keepdims=True)
        squares_hi = squares.astype(BF).astype(F32)
        value_hi = value.astype(BF).astype(F32)
        scaled = value * gain
        scaled = jnp.where(lane == SS_LANE, squares_hi, scaled)
        scaled = jnp.where(lane == SS_LANE + 1, squares - squares_hi, scaled)
        in_hi = jnp.logical_and(lane >= SHARE_HI, lane < SHARE_HI + EXPERTS)
        in_lo = jnp.logical_and(lane >= SHARE_LO, lane < SHARE_LO + EXPERTS)
        scaled = jnp.where(in_hi, value_hi, scaled)
        scaled = jnp.where(in_lo, value - value_hi, scaled)
        rows[s, e] = scaled.astype(BF)
        gather_start(rows.at[s], 8 + s, xy_sem.at[s], r_sem.at[8 + s])

    def arrange():
        wait_bytes(w_r.at[pl.ds(0, NE - 1)], r_sem.at[3])
        pn, pm = iota((LANES, LANES), 0), iota((LANES, LANES), 1)
        pick = jnp.logical_and(pn < SLICE, pm == pn + 2 * (pn // 14)).astype(BF)
        for mat in range(3):
            natural = dot(pick, w_r[:, 16 * mat : 16 * mat + 16, :].reshape(LANES, 256)).astype(BF)
            if mat == 2:
                w_n[2] = natural
            else:
                for half in range(2):
                    w_n[half, :, 128 * mat : 128 * mat + 128] = natural[:, 128 * half : 128 * half + 128]

    ones_at = iota((16, LANES), 1)
    stat_row = jnp.logical_or(ones_at == SS_LANE, ones_at == SS_LANE + 1).astype(BF)
    tail_lane = iota((tokens, 128), 1) + 384
    mine = jnp.logical_or(tail_lane == SHARE_HI + e // 4, tail_lane == SHARE_LO + e // 4)

    def rows_relay(s):
        gather_relay(rows.at[s], 8 + s, xy_sem.at[s], r_sem.at[8 + s])

    def gate(s):
        wait_bytes(rows.at[s, pl.ds(0, NE - NY)], r_sem.at[8 + s])
        flat = rows[s].reshape(tokens, LANES)
        gate_s[s] = dot(flat, w_n[1 - c]).astype(BF)
        remote(gate_s.at[s], gate_r.at[s], s_sem.at[10 + s], r_sem.at[10 + s], sib).start()
        stat = dot_t(stat_row, flat)
        for t in range(4):
            sq_s[s, t] = stat[0:1, 128 * t : 128 * t + 128]
        remote(sq_s.at[s], sq_r.at[s], s_sem.at[12 + s], r_sem.at[12 + s], sib).start()
        gate_o[s] = dot(flat, w_n[c])
        share[s] = jnp.sum(jnp.where(mine, flat[:, 384:].astype(F32), 0.0), axis=1, keepdims=True)

    def z_peer(k):
        t = lax.rem(z + k, NZ)
        return t, {"learn": 2 * t + c}

    def pair_sum(s):
        wait_bytes(gate_r.at[s], r_sem.at[10 + s])
        wait_bytes(sq_r.at[s], r_sem.at[12 + s])
        sum_s[s] = (gate_o[s] + gate_r[s].astype(F32)).astype(BF).reshape(NZ, 64, 256)
        sq_t[s] = sq_s[s] + sq_r[s]
        sum_r[s, z] = sum_s[s, z]
        sq_z[s, z] = sq_t[s, z // 2]

        def send_sum(k, carry):
            t, device = z_peer(k)
            remote(sq_t.at[s, t // 2], sq_z.at[s, z], s_sem.at[16 + s], r_sem.at[16 + s], device).start()
            remote(sum_s.at[s, t], sum_r.at[s, z], s_sem.at[14 + s], r_sem.at[14 + s], device).start()
            return carry

        lax.fori_loop(1, NZ, send_sum, 0)

    sq_row, sq_lane = iota((64, 128), 0), iota((64, 128), 1)
    own_lane = sq_lane == sq_row + 64 * lax.rem(z, 2)

    def activate(s):
        wait_bytes(sum_r.at[s, pl.ds(0, NZ - 1)], r_sem.at[14 + s])
        wait_bytes(sq_z.at[s, pl.ds(0, NZ - 1)], r_sem.at[16 + s])
        total = sum_r[s, 0].astype(F32)
        squares = sq_z[s, 0]
        for k in range(1, NZ):
            total = total + sum_r[s, k].astype(F32)
            squares = squares + sq_z[s, k]
        mean = jnp.sum(jnp.where(own_lane, squares, 0.0), axis=1, keepdims=True) / WIDTH
        total = total * lax.rsqrt(mean + norm_epsilon)
        gated, up = total[:, :128], total[:, 128:]
        acts[s, c, z] = (gated / (1.0 + jnp.exp(-gated)) * up).astype(BF)

        def send_act(k, carry):
            t, device = z_peer(k)
            remote(acts.at[s, c, z], acts.at[s, c, z], s_sem.at[18 + s], r_sem.at[18 + s], device).start()
            return carry

        lax.fori_loop(1, NZ, send_act, 0)

    def pair_acts(s):
        wait_bytes(acts.at[s, c, pl.ds(0, NZ - 1)], r_sem.at[18 + s])
        remote(acts.at[s, c], acts.at[s, c], s_sem.at[20 + s], r_sem.at[20 + s], sib).start()

    def down(s):
        wait_bytes(acts.at[s, 1 - c], r_sem.at[20 + s])
        act = jnp.concatenate(
            [acts[s, 0].reshape(tokens, 128), acts[s, 1].reshape(tokens, 128)], axis=1
        )
        down_s[s] = (dot_t(act, w_n[2]) * share[s]).astype(BF).reshape(NX, 128, LANES)
        down_r[s, x] = down_s[s, x]

        def send_down(k, carry):
            t = lax.rem(x + lax.rem(k, NX - 1) + 1, NX)
            part = pl.ds(pl.multiple_of(k // (NX - 1) * 64, 64), 64)
            remote(
                down_s.at[s, t, part], down_r.at[s, x, part], s_sem.at[22 + s],
                down_sem.at[s, k // (NX - 1)], {"ep": t * NY + y},
            ).start()
            return carry

        lax.fori_loop(0, 2 * (NX - 1), send_down, 0)

    def sum_x(s, half):
        part = pl.ds(64 * half, 64)
        wait_bytes(down_r.at[s, pl.ds(0, NX - 1), part], down_sem.at[s, half])
        total = down_r[s, 0, part].astype(F32)
        for k in range(1, NX):
            total = total + down_r[s, k, part].astype(F32)
        y_s[s, pl.ds(4 * half, 4)] = total.astype(BF).reshape(4, 16, LANES)
        for t in range(4 * half, 4 * half + 4):
            @pl.when(y == t)
            def _():
                y_r[s, t] = y_s[s, t]

            @pl.when(y != t)
            def _():
                remote(
                    y_s.at[s, t], y_r.at[s, y], s_sem.at[24 + s], r_sem.at[24 + s], {"ep": x * NY + t}
                ).start()

    def sum_y(s):
        wait_bytes(y_r.at[s, pl.ds(0, NY - 1)], r_sem.at[24 + s])
        routed = y_r[s, 0].astype(F32)
        for k in range(1, NY):
            routed = routed + y_r[s, k].astype(F32)
        fin_s[:, s, :] = hid[s] + routed

    heads_relay(0)
    heads_relay(1)
    lax.fori_loop(1, NE, send_w, 0)
    project(0)
    project(1)
    move(0)
    wait_bytes(res_r.at[pl.ds(0, NL - 1)], r_sem.at[0])
    rows_start(0)
    move(1)
    rows_relay(0)
    rows_start(1)
    arrange()
    gate(0)
    rows_relay(1)
    pair_sum(0)
    gate(1)
    activate(0)
    pair_sum(1)
    pair_acts(0)
    down(0)
    activate(1)
    sum_x(0, 0)
    sum_x(0, 1)
    pair_acts(1)
    down(1)
    sum_y(0)
    sum_x(1, 0)
    sum_x(1, 1)
    sum_y(1)

    def send_fin(k, carry):
        t = lax.rem(l + k, NL)
        remote(fin_s.at[t], fin_r.at[l], s_sem.at[26], r_sem.at[26], {"learn": t}).start()
        return carry

    lax.fori_loop(1, NL, send_fin, 0)
    fin_r[l] = fin_s[l]
    wait_bytes(fin_r.at[pl.ds(0, NL - 1)], r_sem.at[26])
    for k in range(NL):
        out_ref[:, SLICE * k : SLICE * k + SLICE] = fin_r[k][:, :SLICE]

    wait_bytes(res_r.at[pl.ds(0, NL - 1)], s_sem.at[0])
    wait_bytes(w_r.at[pl.ds(0, NE - 1)], s_sem.at[3])
    wait_bytes(fin_r.at[pl.ds(0, NL - 1)], s_sem.at[26])
    for s in range(STEPS):
        wait_bytes(heads.at[s, pl.ds(0, NE - 1)], s_sem.at[1 + s])
        wait_bytes(att_r.at[s, pl.ds(0, NL - 1)], s_sem.at[4 + s])
        move_wait(s, s_sem.at[6 + s])
        wait_bytes(rows.at[s, pl.ds(0, NE - 1)], s_sem.at[8 + s])
        wait_bytes(gate_s.at[s], s_sem.at[10 + s])
        wait_bytes(sq_s.at[s], s_sem.at[12 + s])
        wait_bytes(sum_s.at[s, pl.ds(0, NZ - 1)], s_sem.at[14 + s])
        wait_bytes(sq_z.at[s, pl.ds(0, NZ - 1)], s_sem.at[16 + s])
        wait_bytes(acts.at[s, 0, pl.ds(0, NZ - 1)], s_sem.at[18 + s])
        wait_bytes(acts.at[s, 0], s_sem.at[20 + s])
        wait_bytes(down_s.at[s, pl.ds(0, NX - 1)], s_sem.at[22 + s])
        wait_bytes(y_s.at[s, pl.ds(0, NY - 1)], s_sem.at[24 + s])


def layer(*operands):
    anywhere = pl.BlockSpec(memory_space=pl.ANY)
    vmem = pl.BlockSpec(memory_space=pltpu.VMEM)
    scratch = [pltpu.VMEM(a.shape, a.dtype) for a in operands] + [
        pltpu.VMEM((NE, 48, 256), BF),
        pltpu.VMEM((2, NE, 16, 256), BF),
        pltpu.VMEM((2, NL, 32, PART), BF),
        pltpu.VMEM((2, NL, 32, PART), BF),
        pltpu.VMEM((2, 2, 16, PART), BF),
        pltpu.VMEM((2, 2, 16, PART), BF),
        pltpu.VMEM((NL, 2, LANES), F32),
        pltpu.VMEM((NL, 2, LANES), F32),
        pltpu.VMEM((2, 16, LANES), F32),
        pltpu.VMEM((2, NE, 16, LANES), BF),
        pltpu.VMEM((NE, 48, 256), BF),
        pltpu.VMEM((3, LANES, 256), BF),
        pltpu.VMEM((2, 512, 256), BF),
        pltpu.VMEM((2, 512, 256), F32),
        pltpu.VMEM((2, 512, 256), BF),
        pltpu.VMEM((2, NZ, 64, 256), BF),
        pltpu.VMEM((2, NZ, 64, 256), BF),
        pltpu.VMEM((2, 4, 1, 128), F32),
        pltpu.VMEM((2, 4, 1, 128), F32),
        pltpu.VMEM((2, 4, 1, 128), F32),
        pltpu.VMEM((2, NZ, 1, 128), F32),
        pltpu.VMEM((2, 2, NZ, 64, 128), BF),
        pltpu.VMEM((2, NX, 128, LANES), BF),
        pltpu.VMEM((2, NX, 128, LANES), BF),
        pltpu.VMEM((2, NY, 16, LANES), BF),
        pltpu.VMEM((2, NY, 16, LANES), BF),
        pltpu.VMEM((NL, 2, LANES), F32),
        pltpu.VMEM((NL, 2, LANES), F32),
        pltpu.VMEM((2, 512, 1), F32),
        pltpu.SemaphoreType.DMA((27,)),
        pltpu.SemaphoreType.DMA((27,)),
        pltpu.SemaphoreType.DMA((2, NY)),
        pltpu.SemaphoreType.DMA((2, NY)),
        pltpu.SemaphoreType.DMA((2, 2)),
        pltpu.SemaphoreType.DMA((15,)),
    ]
    return pl.pallas_call(
        layer_kernel,
        out_shape=jax.ShapeDtypeStruct((2, WIDTH), F32),
        in_specs=[anywhere] * len(operands),
        out_specs=vmem,
        scratch_shapes=scratch,
        compiler_params=pltpu.CompilerParams(
            collective_id=0, has_side_effects=True, vmem_limit_bytes=62 * 2**20
        ),
        name="decode_layer",
    )(*operands)


def per_device(
    master_weight, gradient, first_moment, second_moment, block_slot, queries, kv_cache, new_latent,
    lengths, uv_weight, out_weight, residual, norm_gain, expert_ids, route_weight,
):
    return layer(
        master_weight,
        gradient,
        first_moment,
        second_moment,
        block_slot.reshape(1, NE),
        queries,
        kv_cache.reshape(16 * CACHE, 576),
        new_latent.reshape(32, 576),
        lengths.reshape(1, 16),
        uv_weight,
        jnp.swapaxes(out_weight, 1, 2),
        residual.reshape(2, WIDTH),
        norm_gain.reshape(WIDTH // 128, 128),
        expert_ids,
        route_weight,
    ).reshape(2, 1, WIDTH).astype(BF)


def solution(mesh):
    in_specs = (
        P(("learn", "ep"), None, None, None),
        P(("learn", "ep"), None, None, None),
        P(("learn", "ep"), None, None, None),
        P(("learn", "ep"), None, None, None),
        P(),
        P(None, "ep", "learn", None),
        P("ep", None, None),
        P(None, "ep", None),
        P("ep"),
        P("learn", None, None),
        P("learn", None, "ep"),
        P(None, ("learn", "ep"), None),
        P(),
        P(None, ("learn", "ep"), None),
        P(None, ("learn", "ep"), None),
    )
    out_specs = P(None, ("learn", "ep"), None)
    return jax.shard_map(
        per_device, mesh=mesh, in_specs=in_specs, out_specs=out_specs, check_vma=False
    )
```

time: 135 us -> 106 us (0.79)
  Pallas kernels: 123 us -> 103 us
  local copies, waits for them, and re-layouts: 7.62 us -> 0 us
  other arithmetic: 3.56 us -> 1.45 us
    pallas_call x2 -> x1, Pallas kernels: 123 us -> 103 us  [layer(): pl.pallas_call(layer_kernel, out_shape=jax.ShapeDtypeStruct((2, WIDTH), F...]
    unnamed x15 -> x0, local copies, waits for them, and re-layouts: 3.22 us -> none
    transpose x3 -> x0, local copies, waits for them, and re-layouts: 1.94 us -> none  [the longest x2 1.04 us: per_device(): jnp.transpose(residual.astype(F32).reshape(2, NL, SLICE), (1, 0, 2))]
    reduce_sum x2 -> x0, other arithmetic: 1.55 us -> none  [the longest x1 0.78 us: expert_shares(): jnp.sum(route_weight, axis=-1, keepdims=True)]
    convert_element_type x0 -> x1, other arithmetic: none -> 1.45 us  [per_device(): return layer(master_weight, gradient, first_moment, second_moment, block_...]
where the time goes in v2:
time: 106 us; the launch traced here: 105 us
  Pallas kernels  103 us (97%)
  other arithmetic  1.45 us (1%)
    pallas_call x1, Pallas kernels, layer(): pl.pallas_call(layer_kernel, out_shape=jax.ShapeDtypeStruct((2, WIDTH), F...  103 us

profile of v2, /device:TPU:1, one launch (start us, length us, event | category | flops | bytes accessed | tf_op | source)
XLA Modules:
  0.0 104.8 jit_solution(12276339575642227971)
XLA Ops:
  0.0 103.3 %decode_layer.1 = f32[2,7168]{1,0:T(2,128)} custom-call(f32[14,3,32,256]{3,2,1,0:T(8,128)} %mw_in.1, bf16[14,3,32,256]{3,2,1,0:T(8,128)(2,1)} %gr_in.1, bf16[14,3,32,256]{3,2,1,0:T(8,128)(2,1)} %fm_in.1, bf16[14,3,32,256]{3,2,1,0:T(8,128)(2,1)} %sm_in.1, s32[1,32]{1,0:T(1,128)} %bitcast.14, bf16[2,16,2,576]{3,2,1,0:T(2,128)(2,1)} %q_in.1, ...), custom_call_target="tpu_custom_call" | custom-call | tf_op jit(solution)/shard_map/decode_layer/pallas_call | solution.py:526
  103.3 1.4 %convert_bitcast_fusion = bf16[2,1,7168]{2,0,1:T(2,128)(2,1)} fusion(f32[2,7168]{1,0:T(2,128)} %decode_layer.1), kind=kLoop, calls=%fused_computation | loop fusion | flops 14336 | bytes 86016 | tf_op jit(solution)/shard_map/convert_element_type | solution.py:559

commit v3 on v2

--- a/solution.py
+++ b/solution.py
@@ -59,7 +59,7 @@
     residual_in, gain_in, ids_in, route_in, out_ref,
     mw, gr, fm, sm, slot_ref, q_ref, kv_ref, new_ref, len_ref, uv_ref, ow_ref,
     residual_ref, gain_ref, ids_ref, route_ref,
-    w_s, heads, att_s, att_r, mov_s, mov_r, res_s, res_r, hid, rows, w_r, w_n,
+    w_s, heads, pair_s, pair_r, att_o, att_s, att_r, mov_s, mov_r, res_s, res_r, hid, rows, w_r, w_n,
     gate_s, gate_o, gate_r, sum_s, sum_r, sq_s, sq_r, sq_t, sq_z, acts, down_s, down_r,
     y_s, y_r, fin_s, fin_r, share,
     s_sem, r_sem, hy_sem, xy_sem, down_sem, l_sem,
@@ -169,8 +169,7 @@
         gather_start(heads.at[s], 1 + s, hy_sem.at[s], r_sem.at[1 + s])
 
     pl.semaphore_wait(barrier, NE - 1 + NL - 1 + 2 - own_move.astype(jnp.int32))
-    for s in range(STEPS):
-        heads_start(s)
+    heads_start(0)
 
     for load in loads[5:]:
         load.wait()
@@ -218,36 +217,62 @@
 
     w_r[e] = w_s[e]
 
-    def send_w(k, carry):
+    def send_gates(k, carry):
         t = lax.rem(e + k, NE)
-        remote(w_s.at[t], w_r.at[e], s_sem.at[3], r_sem.at[3], {"ep": t}).start()
+        remote(
+            w_s.at[t, pl.ds(0, 32)], w_r.at[e, pl.ds(0, 32)], s_sem.at[3], r_sem.at[3], {"ep": t}
+        ).start()
         return carry
 
+    def send_downs(k, carry):
+        t = lax.rem(e + k, NE)
+        remote(
+            w_s.at[t, pl.ds(32, 16)], w_r.at[e, pl.ds(32, 16)], s_sem.at[29], r_sem.at[29], {"ep": t}
+        ).start()
+        return carry
+
     tokens = 512
-    n, m = iota((tokens, tokens), 0), iota((tokens, tokens), 1)
-    reorder = (m == 32 * lax.rem(n, 16) + n // 16).astype(BF)
+    n, m = iota((tokens // 2, tokens), 0), iota((tokens // 2, tokens), 1)
+    group = 4 * (n // 32) + lax.rem(n // 16, 2)
+    picked = m - 32 * lax.rem(n, 16) - group
+    reorder_own = (picked == 2 * c).astype(BF)
+    reorder_sib = (picked == 2 - 2 * c).astype(BF)
+
+    def z_peer(k):
+        t = lax.rem(z + k, NZ)
+        return t, {"learn": 2 * t + c}
 
     def heads_relay(s):
         gather_relay(heads.at[s], 1 + s, hy_sem.at[s], r_sem.at[1 + s])
 
     def project(s):
         wait_bytes(heads.at[s, pl.ds(0, NE - NY)], r_sem.at[1 + s])
-        ordered = dot(reorder, heads[s].reshape(tokens, 256)).astype(BF)
-        projected = dot_t(ordered[:, :128], ow_ref[0]) + dot_t(ordered[:, 128:], ow_ref[1])
-        att_s[s] = projected.astype(BF).reshape(NL, 32, PART)
-        att_r[s, l] = att_s[s, l]
+        flat = heads[s].reshape(tokens, 256)
+
+        def half(order):
+            ordered = dot(order, flat).astype(BF)
+            return dot_t(ordered[:, :128], ow_ref[0]) + dot_t(ordered[:, 128:], ow_ref[1])
+
+        pair_s[s] = half(reorder_sib).astype(BF)
+        remote(pair_s.at[s], pair_r.at[s], s_sem.at[27 + s], r_sem.at[27 + s], sib).start()
+        att_o[s] = half(reorder_own)
+
+    def project_sum(s):
+        wait_bytes(pair_r.at[s], r_sem.at[27 + s])
+        att_s[s] = (att_o[s] + pair_r[s].astype(F32)).astype(BF).reshape(NZ, 32, PART)
+        att_r[s, z] = att_s[s, z]
 
         def send_att(k, carry):
-            t = lax.rem(l + k, NL)
-            remote(att_s.at[s, t], att_r.at[s, l], s_sem.at[4 + s], r_sem.at[4 + s], {"learn": t}).start()
+            t, device = z_peer(k)
+            remote(att_s.at[s, t], att_r.at[s, z], s_sem.at[4 + s], r_sem.at[4 + s], device).start()
             return carry
 
-        lax.fori_loop(1, NL, send_att, 0)
+        lax.fori_loop(1, NZ, send_att, 0)
 
     def move(s):
-        wait_bytes(att_r.at[s, pl.ds(0, NL - 1)], r_sem.at[4 + s])
+        wait_bytes(att_r.at[s, pl.ds(0, NZ - 1)], r_sem.at[4 + s])
         total = att_r[s, 0].astype(F32)
-        for k in range(1, NL):
+        for k in range(1, NZ):
             total = total + att_r[s, k].astype(F32)
         mov_s[s] = total.astype(BF).reshape(2, 16, PART)
         for j in range(2):
@@ -301,17 +326,22 @@
         rows[s, e] = scaled.astype(BF)
         gather_start(rows.at[s], 8 + s, xy_sem.at[s], r_sem.at[8 + s])
 
-    def arrange():
-        wait_bytes(w_r.at[pl.ds(0, NE - 1)], r_sem.at[3])
-        pn, pm = iota((LANES, LANES), 0), iota((LANES, LANES), 1)
-        pick = jnp.logical_and(pn < SLICE, pm == pn + 2 * (pn // 14)).astype(BF)
-        for mat in range(3):
-            natural = dot(pick, w_r[:, 16 * mat : 16 * mat + 16, :].reshape(LANES, 256)).astype(BF)
-            if mat == 2:
-                w_n[2] = natural
-            else:
-                for half in range(2):
-                    w_n[half, :, 128 * mat : 128 * mat + 128] = natural[:, 128 * half : 128 * half + 128]
+    pn, pm = iota((LANES, LANES), 0), iota((LANES, LANES), 1)
+    pick = jnp.logical_and(pn < SLICE, pm == pn + 2 * (pn // 14)).astype(BF)
+
+    def natural(mat):
+        return dot(pick, w_r[:, 16 * mat : 16 * mat + 16, :].reshape(LANES, 256)).astype(BF)
+
+    def arrange_gates():
+        wait_bytes(w_r.at[pl.ds(0, NE - 1), pl.ds(0, 32)], r_sem.at[3])
+        for mat in range(2):
+            block = natural(mat)
+            for half in range(2):
+                w_n[half, :, 128 * mat : 128 * mat + 128] = block[:, 128 * half : 128 * half + 128]
+
+    def arrange_downs():
+        wait_bytes(w_r.at[pl.ds(0, NE - 1), pl.ds(32, 16)], r_sem.at[29])
+        w_n[2] = natural(2)
 
     ones_at = iota((16, LANES), 1)
     stat_row = jnp.logical_or(ones_at == SS_LANE, ones_at == SS_LANE + 1).astype(BF)
@@ -332,10 +362,6 @@
         remote(sq_s.at[s], sq_r.at[s], s_sem.at[12 + s], r_sem.at[12 + s], sib).start()
         gate_o[s] = dot(flat, w_n[c])
         share[s] = jnp.sum(jnp.where(mine, flat[:, 384:].astype(F32), 0.0), axis=1, keepdims=True)
-
-    def z_peer(k):
-        t = lax.rem(z + k, NZ)
-        return t, {"learn": 2 * t + c}
 
     def pair_sum(s):
         wait_bytes(gate_r.at[s], r_sem.at[10 + s])
@@ -425,23 +451,28 @@
         fin_s[:, s, :] = hid[s] + routed
 
     heads_relay(0)
+    heads_start(1)
     heads_relay(1)
-    lax.fori_loop(1, NE, send_w, 0)
+    lax.fori_loop(1, NE, send_gates, 0)
     project(0)
+    project_sum(0)
     project(1)
+    project_sum(1)
     move(0)
     wait_bytes(res_r.at[pl.ds(0, NL - 1)], r_sem.at[0])
     rows_start(0)
     move(1)
     rows_relay(0)
     rows_start(1)
-    arrange()
+    arrange_gates()
     gate(0)
     rows_relay(1)
+    lax.fori_loop(1, NE, send_downs, 0)
     pair_sum(0)
     gate(1)
     activate(0)
     pair_sum(1)
+    arrange_downs()
     pair_acts(0)
     down(0)
     activate(1)
@@ -466,11 +497,13 @@
         out_ref[:, SLICE * k : SLICE * k + SLICE] = fin_r[k][:, :SLICE]
 
     wait_bytes(res_r.at[pl.ds(0, NL - 1)], s_sem.at[0])
-    wait_bytes(w_r.at[pl.ds(0, NE - 1)], s_sem.at[3])
+    wait_bytes(w_r.at[pl.ds(0, NE - 1), pl.ds(0, 32)], s_sem.at[3])
+    wait_bytes(w_r.at[pl.ds(0, NE - 1), pl.ds(32, 16)], s_sem.at[29])
     wait_bytes(fin_r.at[pl.ds(0, NL - 1)], s_sem.at[26])
     for s in range(STEPS):
         wait_bytes(heads.at[s, pl.ds(0, NE - 1)], s_sem.at[1 + s])
-        wait_bytes(att_r.at[s, pl.ds(0, NL - 1)], s_sem.at[4 + s])
+        wait_bytes(att_r.at[s, pl.ds(0, NZ - 1)], s_sem.at[4 + s])
+        wait_bytes(pair_s.at[s], s_sem.at[27 + s])
         move_wait(s, s_sem.at[6 + s])
         wait_bytes(rows.at[s, pl.ds(0, NE - 1)], s_sem.at[8 + s])
         wait_bytes(gate_s.at[s], s_sem.at[10 + s])
@@ -489,8 +522,11 @@
     scratch = [pltpu.VMEM(a.shape, a.dtype) for a in operands] + [
         pltpu.VMEM((NE, 48, 256), BF),
         pltpu.VMEM((2, NE, 16, 256), BF),
-        pltpu.VMEM((2, NL, 32, PART), BF),
-        pltpu.VMEM((2, NL, 32, PART), BF),
+        pltpu.VMEM((2, 256, PART), BF),
+        pltpu.VMEM((2, 256, PART), BF),
+        pltpu.VMEM((2, 256, PART), F32),
+        pltpu.VMEM((2, NZ, 32, PART), BF),
+        pltpu.VMEM((2, NZ, 32, PART), BF),
         pltpu.VMEM((2, 2, 16, PART), BF),
         pltpu.VMEM((2, 2, 16, PART), BF),
         pltpu.VMEM((NL, 2, LANES), F32),
@@ -516,8 +552,8 @@
         pltpu.VMEM((NL, 2, LANES), F32),
         pltpu.VMEM((NL, 2, LANES), F32),
         pltpu.VMEM((2, 512, 1), F32),
-        pltpu.SemaphoreType.DMA((27,)),
-        pltpu.SemaphoreType.DMA((27,)),
+        pltpu.SemaphoreType.DMA((30,)),
+        pltpu.SemaphoreType.DMA((30,)),
         pltpu.SemaphoreType.DMA((2, NY)),
         pltpu.SemaphoreType.DMA((2, NY)),
         pltpu.SemaphoreType.DMA((2, 2)),

time: 106 us -> 103 us (0.972)
  Pallas kernels: 103 us -> 101 us
    pallas_call x1, Pallas kernels: 103 us -> 101 us  [layer(): pl.pallas_call(layer_kernel, out_shape=jax.ShapeDtypeStruct((2, WIDTH), F...]
where the time goes in v3:
time: 103 us
  Pallas kernels  101 us (98%)
  other arithmetic  1.45 us (1%)
    pallas_call x1, Pallas kernels, layer(): pl.pallas_call(layer_kernel, out_shape=jax.ShapeDtypeStruct((2, WIDTH), F...  101 us

profile of v3, /device:TPU:1, one launch (start us, length us, event | category | flops | bytes accessed | tf_op | source)
XLA Modules:
  0.0 102.8 jit_solution(13168107830812668314)
XLA Ops:
  0.0 101.3 %decode_layer.1 = f32[2,7168]{1,0:T(2,128)} custom-call(f32[14,3,32,256]{3,2,1,0:T(8,128)} %mw_in.1, bf16[14,3,32,256]{3,2,1,0:T(8,128)(2,1)} %gr_in.1, bf16[14,3,32,256]{3,2,1,0:T(8,128)(2,1)} %fm_in.1, bf16[14,3,32,256]{3,2,1,0:T(8,128)(2,1)} %sm_in.1, s32[1,32]{1,0:T(1,128)} %bitcast.14, bf16[2,16,2,576]{3,2,1,0:T(2,128)(2,1)} %q_in.1, ...), custom_call_target="tpu_custom_call" | custom-call | tf_op jit(solution)/shard_map/decode_layer/pallas_call | solution.py:562
  101.3 1.4 %convert_bitcast_fusion = bf16[2,1,7168]{2,0,1:T(2,128)(2,1)} fusion(f32[2,7168]{1,0:T(2,128)} %decode_layer.1), kind=kLoop, calls=%fused_computation | loop fusion | flops 14336 | bytes 86016 | tf_op jit(solution)/shard_map/convert_element_type | solution.py:595

commit v4 on v3

--- a/solution.py
+++ b/solution.py
@@ -46,6 +46,10 @@
     return pltpu.make_async_remote_copy(
         src_ref=src, dst_ref=dst, send_sem=ssem, recv_sem=rsem, device_id=device, device_id_type=MESH
     )
+
+
+def far_first(k):
+    return jnp.where(lax.rem(k, 2) == 0, 4 - k // 2, 4 + (k - 1) // 2)
 
 
 def column(row, size):
@@ -239,7 +243,7 @@
     reorder_sib = (picked == 2 - 2 * c).astype(BF)
 
     def z_peer(k):
-        t = lax.rem(z + k, NZ)
+        t = lax.rem(z + far_first(k), NZ)
         return t, {"learn": 2 * t + c}
 
     def heads_relay(s):

time: 103 us -> 103 us (level)
  no operation moved by 1% of the time
where the time goes in v4:
time: 103 us; the launch traced here: 102 us
  Pallas kernels  101 us (98%)
  other arithmetic  1.45 us (1%)
    pallas_call x1, Pallas kernels, layer(): pl.pallas_call(layer_kernel, out_shape=jax.ShapeDtypeStruct((2, WIDTH), F...  101 us

profile of v4, /device:TPU:1, one launch (start us, length us, event | category | flops | bytes accessed | tf_op | source)
XLA Modules:
  0.0 102.4 jit_solution(8229098818233313245)
XLA Ops:
  0.0 100.9 %decode_layer.1 = f32[2,7168]{1,0:T(2,128)} custom-call(f32[14,3,32,256]{3,2,1,0:T(8,128)} %mw_in.1, bf16[14,3,32,256]{3,2,1,0:T(8,128)(2,1)} %gr_in.1, bf16[14,3,32,256]{3,2,1,0:T(8,128)(2,1)} %fm_in.1, bf16[14,3,32,256]{3,2,1,0:T(8,128)(2,1)} %sm_in.1, s32[1,32]{1,0:T(1,128)} %bitcast.14, bf16[2,16,2,576]{3,2,1,0:T(2,128)(2,1)} %q_in.1, ...), custom_call_target="tpu_custom_call" | custom-call | tf_op jit(solution)/shard_map/decode_layer/pallas_call | solution.py:566
  101.0 1.4 %convert_bitcast_fusion = bf16[2,1,7168]{2,0,1:T(2,128)(2,1)} fusion(f32[2,7168]{1,0:T(2,128)} %decode_layer.1), kind=kLoop, calls=%fused_computation | loop fusion | flops 14336 | bytes 86016 | tf_op jit(solution)/shard_map/convert_element_type | solution.py:599
